TPU v7x, 32 devices: a whole 2x2x4 slice. The times are simulated.
32 devices in a mesh: dom: 32 (over z, y, x, core).
Axes of the slice: x: 2, y: 2, z: 4, core: 2. Of those that a mesh axis runs over, the one named last changes fastest.
Arguments:
- adjoint_end: bfloat16 [256, 384, 256], P('dom'), may hold values from -6 to 6
- operator_blocks: bfloat16 [256, 6, 384, 384], P('dom'), may hold values from -0.125 to 0.125
- block_cols: int32 [256, 6], P('dom'), may hold values from -1 to 15, as said below
- halo_send: int32 [32, 4, 2], P('dom'), may hold values from -1 to 7, as said below
- wet_cells: int32 [256, 128], P('dom'), may hold values 0 or 1
- gauge_cells: int32 [256], replicated, may hold values from 0 to 32767
- window_first: int32 [256], replicated, may hold values from 0 to 1
- window_len: int32 [256], replicated, may hold values from 1 to 2
- gauge_gain: float32 [256], replicated, may hold values from 0.5 to 4
- snapshots: float32 [2, 256, 384], P(None, 'dom'), may hold values from -27 to 27, as said below
Outputs:
- adjoint_start: bfloat16 [256, 384, 256], P('dom')
- sensitivity: float32 [256, 128, 256], P('dom')
Inputs may be any that keep to these rules, and one draw needn't show every extreme that they name: `block_cols`: in each row entry 0 is the row's own local block; live entries come first and -1 fills the rest; received slots named are only those whose sending device exists. `halo_send`: for each device and neighbour o the 2 blocks are distinct; -1 exactly where device d + off_o does not exist. `snapshots`: nonzero values.
All inputs are finite; a program needn't handle non-finite values. No bound on the sum of `wet_cells` on one device may be relied on, other than what follows from the above.
Results may differ from a plain program's by a relative error of at most 0.0013.
The roundings to bfloat16 on the way count: a program that leaves them out, or rounds other values in their place, can miss the bound.
Values may be sent and summed in bfloat16 or wider, within the bound.
No kernel may reach another device: no remote copies, remote signals or barrier semaphores. Data moves between devices by JAX's collectives and lax.ppermute only.
A program may use at most 128 MiB of HBM per device.

v0:
```python
import jax
import jax.numpy as jnp
from jax import lax
from jax.sharding import PartitionSpec as P

neighbour_offsets = (-2, -1, 1, 2)


def passed_along(value, axis, by):
    devices = lax.axis_size(axis)
    pairs = [(i, i + by) for i in range(devices) if 0 <= i + by < devices]
    return lax.ppermute(value, axis, pairs)


def extended_state(adjoint, send_lists):
    owned = adjoint.shape[0]
    received = [None, None, None, None]
    for group, offset in enumerate(neighbour_offsets):
        received[group] = passed_along(
            adjoint[jnp.clip(send_lists[group], 0, owned - 1)], "dom", offset
        )
    return jnp.concatenate([adjoint] + received, axis=0)


def coupled_rows(extended, operator_blocks, block_cols):
    last = extended.shape[0] - 1
    picked = extended[jnp.clip(block_cols, 0, last)]
    picked = jnp.where((block_cols >= 0)[:, :, None, None], picked, jnp.zeros((), jnp.bfloat16))
    return jnp.einsum("bkij,bkjf->bif", operator_blocks, picked, preferred_element_type=jnp.float32)


def per_device(
    adjoint_end,
    operator_blocks,
    block_cols,
    halo_send,
    wet_cells,
    gauge_cells,
    window_first,
    window_len,
    gauge_gain,
    snapshots,
):
    owned = adjoint_end.shape[0]
    width = adjoint_end.shape[2]
    cell_count = wet_cells.shape[1]
    devices = lax.axis_size("dom")
    position = lax.axis_index("dom")
    send_lists = halo_send[0]
    cell_ids = position * (owned * cell_count) + jnp.arange(
        owned * cell_count, dtype=jnp.int32
    ).reshape(owned, cell_count)
    gauge_hit = (cell_ids[:, :, None] == gauge_cells[None, None, :]).astype(jnp.float32)
    wet_rows = jnp.tile(wet_cells.astype(jnp.float32), (1, 3))[:, :, None]
    padding = jnp.zeros((owned, 2 * cell_count, width), jnp.float32)
    adjoint = adjoint_end
    raw = jnp.zeros((owned, cell_count, width), jnp.float32)
    for step_index in range(snapshots.shape[0]):
        extended = extended_state(adjoint, send_lists)
        coupled = coupled_rows(extended, operator_blocks, block_cols)
        active = ((window_first <= step_index) & (step_index < window_first + window_len)).astype(
            jnp.float32
        ) * gauge_gain
        source_full = jnp.concatenate([gauge_hit * active[None, None, :], padding], axis=1)
        updated = wet_rows * (adjoint.astype(jnp.float32) + coupled) + source_full
        adjoint = updated.astype(jnp.bfloat16)
        saved = snapshots[step_index].reshape(owned, 3, cell_count)[:, :, :, None]
        raw = raw + jnp.sum(
            saved * adjoint.astype(jnp.float32).reshape(owned, 3, cell_count, width), axis=1
        )
    totals = lax.psum(jnp.sum(raw * raw, axis=(0, 1)), "dom")
    meansq = totals / (devices * owned * cell_count)
    sensitivity = raw * lax.rsqrt(meansq + 1e-06)[None, None, :]
    return (adjoint, sensitivity)


def solution(mesh):
    return jax.shard_map(
        per_device,
        mesh=mesh,
        in_specs=(
            P("dom", None, None),
            P("dom", None, None, None),
            P("dom", None),
            P("dom", None, None),
            P("dom", None),
            P(),
            P(),
            P(),
            P(),
            P(None, "dom", None),
        ),
        out_specs=(P("dom", None, None), P("dom", None, None)),
        check_vma=False,
    )
```

profile of v0, /device:TPU:0, one launch (start us, length us, event | category | flops | bytes accessed | tf_op | source)
XLA Modules:
  0.0 179.2 jit_solution(7408783445713412860)
XLA Ops:
  0.7 1.0 clamp_reduce_fusion
  1.8 2.7 %gather_fusion = bf16[2,384,256]{2,1,0:T(8,128)(2,1)} fusion(bf16[8,384,256]{2,1,0:T(8,128)(2,1)} %param.10, s32[1024]{0:T(1024)S(1)} %pad_clamp_fusion.4), kind=kCustom, calls=%fused_computation | custom fusion | bytes 786440 | tf_op jit(solution)/shard_map/gather | solution.py:20
  4.5 1.3 collective-permute-start
  5.8 2.7 %gather_fusion.1 = bf16[2,384,256]{2,1,0:T(8,128)(2,1)} fusion(bf16[8,384,256]{2,1,0:T(8,128)(2,1)} %param.10, s32[1024]{0:T(1024)S(1)} %pad_clamp_fusion.3), kind=kCustom, calls=%fused_computation.1 | custom fusion | bytes 786440 | tf_op jit(solution)/shard_map/gather | solution.py:20
  8.5 1.3 collective-permute-start.1
  9.9 2.7 %gather_fusion.2 = bf16[2,384,256]{2,1,0:T(8,128)(2,1)} fusion(bf16[8,384,256]{2,1,0:T(8,128)(2,1)} %param.10, s32[1024]{0:T(1024)S(1)} %pad_clamp_fusion.2), kind=kCustom, calls=%fused_computation.2 | custom fusion | bytes 786440 | tf_op jit(solution)/shard_map/gather | solution.py:20
  12.6 3.8 %collective-permute-start.2 = (bf16[2,384,256]{2,1,0:T(8,128)(2,1)}, bf16[2,384,256]{2,1,0:T(8,128)(2,1)}, u32[]{:S(2)}, u32[]{:S(2)}) collective-permute-start(bf16[2,384,256]{2,1,0:T(8,128)(2,1)} %gather_fusion.2), channel_id=1, source_target_pairs={{0,1},{1,2},{2,3},{3,4},{4,5},{5,6},{6,7},{7,8},{8,9},{9,10},{10,1... | collective-permute-start | bytes 1179656 | tf_op jit(solution)/shard_map/ppermute | solution.py:12
  16.4 2.7 %gather_fusion.3 = bf16[2,384,256]{2,1,0:T(8,128)(2,1)} fusion(bf16[8,384,256]{2,1,0:T(8,128)(2,1)} %param.10, s32[1024]{0:T(1024)S(1)} %pad_clamp_fusion.1), kind=kCustom, calls=%fused_computation.3 | custom fusion | bytes 786440 | tf_op jit(solution)/shard_map/gather | solution.py:20
  19.1 5.5 %collective-permute-start.3 = (bf16[2,384,256]{2,1,0:T(8,128)(2,1)}, bf16[2,384,256]{2,1,0:T(8,128)(2,1)}, u32[]{:S(2)}, u32[]{:S(2)}) collective-permute-start(bf16[2,384,256]{2,1,0:T(8,128)(2,1)} %gather_fusion.3), channel_id=1, source_target_pairs={{0,2},{1,3},{2,4},{3,5},{4,6},{5,7},{6,8},{7,9},{8,10},{9,11},{10,... | collective-permute-start | bytes 1179656 | tf_op jit(solution)/shard_map/ppermute | solution.py:12
  24.7 1.6 compare_select_fusion.1
  28.3 2.6 %copy.17 = bf16[8,384,256]{1,2,0:T(8,128)(2,1)} copy(bf16[8,384,256]{2,1,0:T(8,128)(2,1)} %param.10) | data formatting | bytes 3145728 | tf_op args[0]
  34.8 6.3 %gather_fusion.4 = bf16[48,384,256]{2,1,0:T(8,128)(2,1)} fusion(bf16[16,384,256]{2,1,0:T(8,128)(2,1)S(1)} %constant_dynamic-update-slice_fusion, s32[1024]{0:T(1024)S(1)} %pad_clamp_fusion), kind=kCustom, calls=%fused_computation.4 | custom fusion | bytes 18874560 | tf_op jit(solution)/shard_map/gather | solution.py:27
  41.1 12.6 %copy.18 = bf16[8,6,384,256]{2,3,1,0:T(8,128)(2,1)} copy(bf16[8,6,384,256]{3,2,1,0:T(8,128)(2,1)} %bitcast.50) | data formatting | bytes 18874368 | tf_op jit(solution)/shard_map/gather | solution.py:27
  53.7 12.2 %constant_dynamic-update-slice_fusion.9 = (bf16[16,384,256]{1,2,0:T(8,128)(2,1)S(1)}, bf16[8,384,256]{1,2,0:T(8,128)(2,1)}) fusion(f32[8,128,256]{1,2,0:T(8,128)} %get-tuple-element.14, bf16[8,6,384,384]{3,2,1,0:T(8,128)(2,1)} %param.11, bf16[8,6,384,256]{2,3,1,0:T(8,128)(2,1)} %copy.18, pred[8,6]{1,0:T(8,128)(4,1)S(1)} %copy-done.15, ...), kind=kOutput, calls=%fused_computation.41 | convolution fusion | flops 3632529408 | bytes 29372464 | tf_op jit(solution)/shard_map/bkij,bkjf->bif/dot_general | solution.py:29
  65.9 2.9 %gather_fusion.5 = bf16[2,384,256]{1,2,0:T(8,128)(2,1)} fusion(bf16[8,384,256]{1,2,0:T(8,128)(2,1)} %get-tuple-element.19, s32[1024]{0:T(1024)} %copy-done.6), kind=kCustom, calls=%fused_computation.5 | custom fusion | bytes 786440 | tf_op jit(solution)/shard_map/gather | solution.py:20
  68.8 2.9 %gather_fusion.6 = bf16[2,384,256]{1,2,0:T(8,128)(2,1)} fusion(bf16[8,384,256]{1,2,0:T(8,128)(2,1)} %get-tuple-element.19, s32[1024]{0:T(1024)} %copy-done.8), kind=kCustom, calls=%fused_computation.6 | custom fusion | bytes 786440 | tf_op jit(solution)/shard_map/gather | solution.py:20
  71.6 1.3 collective-permute-start.4
  72.9 1.3 collective-permute-start.5
  75.6 2.9 %gather_fusion.7 = bf16[2,384,256]{1,2,0:T(8,128)(2,1)} fusion(bf16[8,384,256]{1,2,0:T(8,128)(2,1)} %get-tuple-element.19, s32[1024]{0:T(1024)} %copy-done.7), kind=kCustom, calls=%fused_computation.7 | custom fusion | bytes 786440 | tf_op jit(solution)/shard_map/gather | solution.py:20
  78.5 2.9 %gather_fusion.8 = bf16[2,384,256]{1,2,0:T(8,128)(2,1)} fusion(bf16[8,384,256]{1,2,0:T(8,128)(2,1)} %get-tuple-element.19, s32[1024]{0:T(1024)} %copy-done.9), kind=kCustom, calls=%fused_computation.8 | custom fusion | bytes 786440 | tf_op jit(solution)/shard_map/gather | solution.py:20
  81.3 3.0 %copy.20 = f32[8,384,256]{2,1,0:T(8,128)} copy(bf16[8,384,256]{1,2,0:T(8,128)(2,1)} %get-tuple-element.19) | data formatting | bytes 4718592 | tf_op jit(solution)/shard_map/convert_element_type | solution.py:65
  84.4 5.7 %collective-permute-start.6 = (bf16[2,384,256]{1,2,0:T(8,128)(2,1)}, bf16[2,384,256]{1,2,0:T(8,128)(2,1)S(1)}, u32[]{:S(2)}, u32[]{:S(2)}) collective-permute-start(bf16[2,384,256]{1,2,0:T(8,128)(2,1)} %gather_fusion.7), channel_id=1, source_target_pairs={{0,1},{1,2},{2,3},{3,4},{4,5},{5,6},{6,7},{7,8},{8,9},{9,10},{10,1... | collective-permute-start | bytes 1179656 | tf_op jit(solution)/shard_map/ppermute | solution.py:12
  90.1 4.8 %collective-permute-start.7 = (bf16[2,384,256]{1,2,0:T(8,128)(2,1)}, bf16[2,384,256]{1,2,0:T(8,128)(2,1)S(1)}, u32[]{:S(2)}, u32[]{:S(2)}) collective-permute-start(bf16[2,384,256]{1,2,0:T(8,128)(2,1)} %gather_fusion.8), channel_id=1, source_target_pairs={{0,2},{1,3},{2,4},{3,5},{4,6},{5,7},{6,8},{7,9},{8,10},{9,11},{10,... | collective-permute-start | bytes 1179656 | tf_op jit(solution)/shard_map/ppermute | solution.py:12
  94.9 3.4 %multiply_reduce_fusion.1 = f32[8,128,256]{2,1,0:T(8,128)} fusion(f32[8,3,128,256]{3,2,1,0:T(8,128)} %bitcast.51, f32[8,3,128]{2,1,0:T(4,128)} %copy.19), kind=kLoop, calls=%fused_computation.27 | loop fusion | flops 1310720 | bytes 4206592 | tf_op jit(solution)/shard_map/reduce_sum | solution.py:68
  98.3 1.1 constant_dynamic-update-slice_fusion.8
  99.6 4.8 %collective-permute-done.7 = bf16[2,384,256]{1,2,0:T(8,128)(2,1)S(1)} collective-permute-done((bf16[2,384,256]{1,2,0:T(8,128)(2,1)}, bf16[2,384,256]{1,2,0:T(8,128)(2,1)S(1)}, u32[]{:S(2)}, u32[]{:S(2)}) %collective-permute-start.7) | collective-permute-done | bytes 393248 | tf_op jit(solution)/shard_map/ppermute | solution.py:12
  104.5 6.8 %gather_fusion.9 = bf16[48,384,256]{1,2,0:T(8,128)(2,1)} fusion(bf16[16,384,256]{1,2,0:T(8,128)(2,1)S(1)} %constant_dynamic-update-slice_fusion.5, s32[1024]{0:T(1024)} %copy-done.2), kind=kCustom, calls=%fused_computation.9 | custom fusion | bytes 18874560 | tf_op jit(solution)/shard_map/gather | solution.py:27
  111.3 16.3 %fusion.10 = bf16[8,384,256]{1,2,0:T(8,128)(2,1)} fusion(f32[8,128,256]{1,2,0:T(8,128)} %get-tuple-element.15, bf16[8,6,384,384]{3,2,1,0:T(8,128)(2,1)} %param.11, bf16[8,6,384,256]{2,3,1,0:T(8,128)(2,1)} %bitcast.53, pred[8,6]{1,0:T(8,128)(4,1)S(1)} %copy-done.16, f32[8,384]{1,0:T(8,128)S(1)} %copy-done.5, bf16[8,384,256]{1,2,0:T(8,128)(2,1)} %get-tuple-element.19), kind=kOutput, calls=%fused_computation.21 | convolution fusion | flops 3632529408 | bytes 27799600 | tf_op jit(solution)/shard_map/bkij,bkjf->bif/dot_general | solution.py:29
  127.6 1.7 copy.22
  129.3 2.6 %copy.23 = bf16[8,384,256]{2,1,0:T(8,128)(2,1)} copy(bf16[8,384,256]{1,2,0:T(8,128)(2,1)} %fusion.10) | data formatting | bytes 3145728
  133.4 44.8 %psum.7 = f32[256]{0:T(256)S(1)} all-reduce(f32[256]{0:T(256)S(1)} %get-tuple-element.10), channel_id=1, replica_groups=mesh['dom'=32] {'dom'}, use_global_device_ids=true, to_apply=%region_3.4 | all-reduce | flops 256 | bytes 2048 | tf_op jit(solution)/shard_map/psum | solution.py:71
  178.1 1.1 broadcast_multiply_fusion
  (69 shorter events, 8.9 us)
Async XLA Ops:
  0.6 24.0 %copy-start.3 = (s32[8,6]{1,0:T(8,128)S(1)}, s32[8,6]{1,0:T(8,128)}, u32[]{:S(2)}) copy-start(s32[8,6]{1,0:T(8,128)} %param.12) | copy-start | bytes 580
  0.6 24.0 %copy-start.10 = (s32[8,128]{1,0:T(8,128)S(1)}, s32[8,128]{1,0:T(8,128)}, u32[]{:S(2)}) copy-start(s32[8,128]{1,0:T(8,128)} %param.14) | copy-start | bytes 12292
  0.7 24.0 %copy-start.13 = (s32[256]{0:T(256)S(1)}, s32[256]{0:T(256)}, u32[]{:S(2)}) copy-start(s32[256]{0:T(256)} %param.16) | copy-start | bytes 3076
  0.7 24.0 %copy-start.14 = (s32[256]{0:T(256)S(1)}, s32[256]{0:T(256)}, u32[]{:S(2)}) copy-start(s32[256]{0:T(256)} %param.17) | copy-start | bytes 3076
  0.7 24.0 %copy-start.12 = (f32[256]{0:T(256)S(1)}, f32[256]{0:T(256)}, u32[]{:S(2)}) copy-start(f32[256]{0:T(256)} %param.18) | copy-start | bytes 3076
  0.7 24.1 %copy-start.11 = (s32[256]{0:T(256)S(1)}, s32[256]{0:T(256)}, u32[]{:S(2)}) copy-start(s32[256]{0:T(256)} %param.15) | copy-start | bytes 3076
  1.8 22.9 %copy-start.6 = (s32[1024]{0:T(1024)}, s32[1024]{0:T(1024)S(1)}, u32[]{:S(2)}) copy-start(s32[1024]{0:T(1024)S(1)} %pad_clamp_fusion.4) | copy-start | bytes 12292
  4.5 26.4 %collective-permute-start = (bf16[2,384,256]{2,1,0:T(8,128)(2,1)}, bf16[2,384,256]{2,1,0:T(8,128)(2,1)S(1)}, u32[]{:S(2)}, u32[]{:S(2)}) collective-permute-start(bf16[2,384,256]{2,1,0:T(8,128)(2,1)} %gather_fusion), channel_id=1, source_target_pairs={{2,0},{3,1},{4,2},{5,3},{6,4},{7,5},{8,6},{9,7},{10,8},{11,9},{12,... | collective-permute-start | bytes 1179656 | tf_op jit(solution)/shard_map/ppermute | solution.py:12
  5.8 4.0 %copy-start.8 = (s32[1024]{0:T(1024)}, s32[1024]{0:T(1024)S(1)}, u32[]{:S(2)}) copy-start(s32[1024]{0:T(1024)S(1)} %pad_clamp_fusion.3) | copy-start | bytes 12292
  8.5 22.4 %collective-permute-start.1 = (bf16[2,384,256]{2,1,0:T(8,128)(2,1)}, bf16[2,384,256]{2,1,0:T(8,128)(2,1)}, u32[]{:S(2)}, u32[]{:S(2)}) collective-permute-start(bf16[2,384,256]{2,1,0:T(8,128)(2,1)} %gather_fusion.1), channel_id=1, source_target_pairs={{1,0},{2,1},{3,2},{4,3},{5,4},{6,5},{7,6},{8,7},{9,8},{10,9},{11,1... | collective-permute-start | bytes 1179656 | tf_op jit(solution)/shard_map/ppermute | solution.py:12
  9.8 16.5 %copy-start.7 = (s32[1024]{0:T(1024)}, s32[1024]{0:T(1024)S(1)}, u32[]{:S(2)}) copy-start(s32[1024]{0:T(1024)S(1)} %pad_clamp_fusion.2) | copy-start | bytes 12292
  12.6 19.4 %collective-permute-start.2 = (bf16[2,384,256]{2,1,0:T(8,128)(2,1)}, bf16[2,384,256]{2,1,0:T(8,128)(2,1)}, u32[]{:S(2)}, u32[]{:S(2)}) collective-permute-start(bf16[2,384,256]{2,1,0:T(8,128)(2,1)} %gather_fusion.2), channel_id=1, source_target_pairs={{0,1},{1,2},{2,3},{3,4},{4,5},{5,6},{6,7},{7,8},{8,9},{9,10},{10,1... | collective-permute-start | bytes 1179656 | tf_op jit(solution)/shard_map/ppermute | solution.py:12
  16.4 10.0 %copy-start.9 = (s32[1024]{0:T(1024)}, s32[1024]{0:T(1024)S(1)}, u32[]{:S(2)}) copy-start(s32[1024]{0:T(1024)S(1)} %pad_clamp_fusion.1) | copy-start | bytes 12292
  19.1 14.6 %collective-permute-start.3 = (bf16[2,384,256]{2,1,0:T(8,128)(2,1)}, bf16[2,384,256]{2,1,0:T(8,128)(2,1)}, u32[]{:S(2)}, u32[]{:S(2)}) collective-permute-start(bf16[2,384,256]{2,1,0:T(8,128)(2,1)} %gather_fusion.3), channel_id=1, source_target_pairs={{0,2},{1,3},{2,4},{3,5},{4,6},{5,7},{6,8},{7,9},{8,10},{9,11},{10,... | collective-permute-start | bytes 1179656 | tf_op jit(solution)/shard_map/ppermute | solution.py:12
  24.6 2.3 %copy-start = (bf16[8,384,256]{2,1,0:T(8,128)(2,1)S(1)}, bf16[8,384,256]{2,1,0:T(8,128)(2,1)}, u32[]{:S(2)}) copy-start(bf16[8,384,256]{2,1,0:T(8,128)(2,1)} %param.10) | copy-start | bytes 4718596
  24.7 29.0 %copy-start.4 = (f32[8,384]{1,0:T(8,128)}, f32[8,384]{1,0:T(8,128)S(1)}, u32[]{:S(2)}) copy-start(f32[8,384]{1,0:T(8,128)S(1)} %broadcast_bitcast_fusion) | copy-start | bytes 36868
  28.3 6.5 %copy-start.2 = (s32[1024]{0:T(1024)}, s32[1024]{0:T(1024)S(1)}, u32[]{:S(2)}) copy-start(s32[1024]{0:T(1024)S(1)} %pad_clamp_fusion) | copy-start | bytes 12292
  41.1 12.6 %copy-start.15 = (pred[8,6]{1,0:T(8,128)(4,1)S(1)}, pred[8,6]{1,0:T(8,128)(4,1)}, u32[]{:S(2)}) copy-start(pred[8,6]{1,0:T(8,128)(4,1)} %broadcast_compare_fusion) | copy-start | bytes 148
  71.6 26.7 %collective-permute-start.4 = (bf16[2,384,256]{1,2,0:T(8,128)(2,1)}, bf16[2,384,256]{1,2,0:T(8,128)(2,1)}, u32[]{:S(2)}, u32[]{:S(2)}) collective-permute-start(bf16[2,384,256]{1,2,0:T(8,128)(2,1)} %gather_fusion.5), channel_id=1, source_target_pairs={{2,0},{3,1},{4,2},{5,3},{6,4},{7,5},{8,6},{9,7},{10,8},{11,9},{12,... | collective-permute-start | bytes 1179656 | tf_op jit(solution)/shard_map/ppermute | solution.py:12
  72.9 26.5 %collective-permute-start.5 = (bf16[2,384,256]{1,2,0:T(8,128)(2,1)}, bf16[2,384,256]{1,2,0:T(8,128)(2,1)S(1)}, u32[]{:S(2)}, u32[]{:S(2)}) collective-permute-start(bf16[2,384,256]{1,2,0:T(8,128)(2,1)} %gather_fusion.6), channel_id=1, source_target_pairs={{1,0},{2,1},{3,2},{4,3},{5,4},{6,5},{7,6},{8,7},{9,8},{10,9},{11,1... | collective-permute-start | bytes 1179656 | tf_op jit(solution)/shard_map/ppermute | solution.py:12
  84.4 15.1 %collective-permute-start.6 = (bf16[2,384,256]{1,2,0:T(8,128)(2,1)}, bf16[2,384,256]{1,2,0:T(8,128)(2,1)S(1)}, u32[]{:S(2)}, u32[]{:S(2)}) collective-permute-start(bf16[2,384,256]{1,2,0:T(8,128)(2,1)} %gather_fusion.7), channel_id=1, source_target_pairs={{0,1},{1,2},{2,3},{3,4},{4,5},{5,6},{6,7},{7,8},{8,9},{9,10},{10,1... | collective-permute-start | bytes 1179656 | tf_op jit(solution)/shard_map/ppermute | solution.py:12
  90.1 14.2 %collective-permute-start.7 = (bf16[2,384,256]{1,2,0:T(8,128)(2,1)}, bf16[2,384,256]{1,2,0:T(8,128)(2,1)S(1)}, u32[]{:S(2)}, u32[]{:S(2)}) collective-permute-start(bf16[2,384,256]{1,2,0:T(8,128)(2,1)} %gather_fusion.8), channel_id=1, source_target_pairs={{0,2},{1,3},{2,4},{3,5},{4,6},{5,7},{6,8},{7,9},{8,10},{9,11},{10,... | collective-permute-start | bytes 1179656 | tf_op jit(solution)/shard_map/ppermute | solution.py:12
  104.4 6.8 %copy-start.5 = (f32[8,384]{1,0:T(8,128)S(1)}, f32[8,384]{1,0:T(8,128)}, u32[]{:S(2)}) copy-start(f32[8,384]{1,0:T(8,128)} %copy-done.4) | copy-start | bytes 36868
  104.4 6.8 %copy-start.16 = (pred[8,6]{1,0:T(8,128)(4,1)S(1)}, pred[8,6]{1,0:T(8,128)(4,1)}, u32[]{:S(2)}) copy-start(pred[8,6]{1,0:T(8,128)(4,1)} %broadcast_compare_fusion) | copy-start | bytes 148
  131.9 1.2 copy-start.1
where the time goes:
time: 181 us; the launch traced here: 179 us
  local copies, waits for them, and re-layouts  65.3 us (36%)
  blocking collectives  44.8 us (25%)
  matrix products  28.6 us (16%)
  starting transfers between devices  24.9 us (14%)
  other arithmetic  9.13 us (5%)
  waiting for transfers between devices  5.54 us (3%)
    psum x1, blocking collectives, per_device(): totals = lax.psum(jnp.sum(raw * raw, axis=(0, 1)), 'dom')  44.8 us
    dot_general x2, matrix products, coupled_rows(): jnp.einsum('bkij,bkjf->bif', operator_blocks, picked, preferred_element_t...  28.6 us
    gather x3, local copies, waits for them, and re-layouts, coupled_rows(): picked = extended[jnp.clip(block_cols, 0, last)]  25.7 us
    ppermute x8, starting transfers between devices, passed_along(): return lax.ppermute(value, axis, pairs)  24.9 us
    gather x8, local copies, waits for them, and re-layouts, extended_state(): adjoint[jnp.clip(send_lists[group], 0, owned - 1)]  22.4 us
    unnamed x43, local copies, waits for them, and re-layouts  9.34 us
    ppermute x8, waiting for transfers between devices, passed_along(): return lax.ppermute(value, axis, pairs)  5.54 us
    reduce_sum x2, other arithmetic, per_device(): jnp.sum(saved * adjoint.astype(jnp.float32).reshape(owned, 3, cell_count,...  3.87 us
  transfers between devices with their start and end apart: 8, of which 2 were waited for; matrix products, arithmetic and copies ran while one was open for 17% of the time, Pallas kernels for 0%

commit v1 on v0

v1 whole, which is shorter than its diff:
```python
import functools

import jax
import jax.numpy as jnp
from jax import lax
from jax.experimental import pallas as pl
from jax.experimental.pallas import tpu as pltpu
from jax.sharding import PartitionSpec as P

ROUTES = ("swap", "cross", "inner", "outer")


def route_pairs(devices):
    swap = [(i, i ^ 1) for i in range(devices)]
    cross = [(i, i + 1) for i in range(1, devices - 1, 2)]
    inner = [(i, i ^ 2) for i in range(devices)]
    outer = [(i, i + 2) for i in range(devices - 2) if i & 2]
    both = lambda pairs: pairs + [(j, i) for i, j in pairs]
    return dict(swap=swap, cross=both(cross), inner=inner, outer=both(outer))


def send_groups(device):
    core, chip = device % 2, (device // 2) % 2
    return dict(swap=2 - core, cross=1 + core, inner=3 - 3 * chip, outer=3 * chip)


def receive_groups(device):
    core, chip = device % 2, (device // 2) % 2
    return dict(swap=1 + core, cross=2 - core, inner=3 * chip, outer=3 - 3 * chip)


def exchange(sends):
    pairs = route_pairs(lax.axis_size("dom"))
    return {r: lax.ppermute(sends[r], "dom", pairs[r]) for r in ("inner", "cross", "outer", "swap")}


def pick_kernel(halo, lam, *rest):
    outs, sems = dict(zip(ROUTES, rest[:4])), rest[4]
    groups = send_groups(lax.axis_index("dom"))
    copies = []
    for i, r in enumerate(ROUTES):
        for c in range(2):
            row = jnp.maximum(halo[groups[r], c], 0)
            copies.append(pltpu.make_async_copy(lam.at[row], outs[r].at[c], sems.at[i, c]))
    for copy in copies:
        copy.start()
    for copy in copies:
        copy.wait()


def pick_sends(halo, lam):
    part = jax.ShapeDtypeStruct((2,) + lam.shape[1:], lam.dtype)
    outs = pl.pallas_call(
        pick_kernel,
        name="pick_sends",
        out_shape=[part] * 4,
        in_specs=[pl.BlockSpec(memory_space=pltpu.SMEM), pl.BlockSpec(memory_space=pl.ANY)],
        out_specs=[pl.BlockSpec(memory_space=pl.ANY)] * 4,
        scratch_shapes=[pltpu.SemaphoreType.DMA((4, 2))],
    )(halo, lam)
    return dict(zip(ROUTES, outs))


def step_kernel(late, last, step, devices, *refs):
    refs = list(refs)
    take = lambda n: [refs.pop(0) for _ in range(n)]
    cols, halo, lam, ops, aux, gauges = take(6)
    received = take(4) if late else []
    (done,) = take(1) if late else (None,)
    done_raw, done_squares = take(2) if late and last else (None, None)
    (new,) = take(1)
    raw, squares = take(2) if last else (None, None)
    sends = dict(zip(ROUTES, take(4))) if late and not last else {}
    ext, opbuf, out, rawbuf, ext_sem, op_sem, out_sem, raw_sem, send_sem, flags = refs

    owned, entries = ops.shape[0], ops.shape[1]
    rows, width = lam.shape[1], lam.shape[2]
    cells = rows // 3
    zero_block = ext.shape[0] - 1
    position = lax.axis_index("dom")

    def pairs_of(b):
        live = 0
        for k in range(entries):
            live = live + (cols[b, k] >= 0).astype(jnp.int32)
        return (live + 1) // 2

    def is_mine(b):
        top = cols[b, 0]
        for k in range(1, entries):
            top = jnp.maximum(top, cols[b, k])
        return (top >= owned) if late else (top < owned)

    copies = [pltpu.make_async_copy(lam, ext.at[pl.ds(0, owned)], ext_sem.at[4])]
    if late:
        groups = receive_groups(position)
        for i, r in enumerate(ROUTES):
            copies.append(
                pltpu.make_async_copy(received[i], ext.at[pl.ds(owned + 2 * groups[r], 2)], ext_sem.at[i])
            )

    def op_copy(b, p):
        return pltpu.make_async_copy(
            ops.at[b, pl.ds(2 * p, 2)], opbuf.at[b, pl.ds(2 * p, 2)], op_sem.at[b, p]
        )

    for copy in copies:
        copy.start()

    @pl.loop(0, owned)
    def _(b):
        mine = is_mine(b)
        number = pairs_of(b)
        flags[b] = jnp.where(mine, number, 0)
        for p in range(entries // 2):

            @pl.when(jnp.logical_and(mine, number > p))
            def _():
                op_copy(b, p).start()

    send_rows = []
    if sends:
        groups = send_groups(position)
        for i, r in enumerate(ROUTES):
            for c in range(2):
                send_rows.append((i, r, c, jnp.maximum(halo[groups[r], c], 0)))
        for i, r, c, row in send_rows:

            @pl.when(flags[row] == 0)
            def _(i=i, r=r, c=c, row=row):
                pltpu.make_async_copy(done.at[row], sends[r].at[c], send_sem.at[i, c]).start()

    ext[zero_block] = jnp.zeros((rows, width), ext.dtype)
    if last:
        if late:
            squares[...] = jnp.broadcast_to(done_squares[...], squares.shape)
        else:
            squares[...] = jnp.zeros(squares.shape, jnp.float32)
    for copy in copies:
        copy.wait()

    first = gauges[1:2, :]
    active = jnp.where(
        jnp.logical_and(first <= step, step < first + gauges[2:3, :]), gauges[3:4, :], 0.0
    )
    own_cells = lax.broadcasted_iota(jnp.int32, (cells, width), 0)

    def finish(b, total):
        wet = aux[b, :, 0:1]
        where = gauges[0:1, :].astype(jnp.int32) - (position * owned + b) * cells
        source = jnp.where(own_cells == where, active, 0.0)
        gathered = None
        for c in range(3):
            part = pl.ds(c * cells, cells)
            before = ext[b, part, :].astype(jnp.float32)
            updated = wet * (before + total[c * cells : (c + 1) * cells])
            if c == 0:
                updated = updated + source
            updated = updated.astype(jnp.bfloat16)
            out[b, part, :] = updated
            if last:
                term = aux[b, :, 1 + c : 2 + c] * before
                gathered = term if gathered is None else gathered + term
                gathered = gathered + aux[b, :, 4 + c : 5 + c] * updated.astype(jnp.float32)
        if last:
            rawbuf[b] = gathered
            squares[...] += jnp.broadcast_to(
                jnp.sum(gathered * gathered, axis=0, keepdims=True), squares.shape
            )

    @pl.loop(0, owned)
    def _(b):
        number = flags[b]

        for n in range(1, entries // 2 + 1):

            @pl.when(number == n)
            def _(n=n):
                for p in range(n):
                    op_copy(b, p).wait()
                picked = []
                for k in range(2 * n):
                    col = cols[b, k]
                    picked.append(ext[jnp.where(col < 0, zero_block, col)])
                weights = jnp.concatenate([opbuf[b, k] for k in range(2 * n)], axis=1)
                total = jnp.dot(
                    weights, jnp.concatenate(picked, axis=0), preferred_element_type=jnp.float32
                )
                finish(b, total)

        @pl.when(number > 0)
        def _():
            pltpu.make_async_copy(out.at[b], new.at[b], out_sem.at[b]).start()
            if last:
                pltpu.make_async_copy(rawbuf.at[b], raw.at[b], raw_sem.at[b]).start()
            for i, r, c, row in send_rows:

                @pl.when(row == b)
                def _(i=i, r=r, c=c):
                    pltpu.make_async_copy(out.at[b], sends[r].at[c], send_sem.at[i, c]).start()

    @pl.loop(0, owned)
    def _(b):
        @pl.when(flags[b] > 0)
        def _():
            pltpu.make_async_copy(out.at[b], new.at[b], out_sem.at[b]).wait()
            if last:
                pltpu.make_async_copy(rawbuf.at[b], raw.at[b], raw_sem.at[b]).wait()

    for i, r, c, row in send_rows:
        pltpu.make_async_copy(out.at[0], sends[r].at[c], send_sem.at[i, c]).wait()


def step_rows(late, last, step, cols, halo, lam, ops, aux, gauges, received=None, early=None):
    owned, rows, width = lam.shape
    cells = rows // 3
    devices = lax.axis_size("dom")
    smem, vmem, hbm = (pl.BlockSpec(memory_space=m) for m in (pltpu.SMEM, pltpu.VMEM, pl.ANY))
    args = [cols, halo, lam, ops, aux, gauges]
    in_specs = [smem, smem, hbm, hbm, vmem, vmem]
    aliases = {}
    if late:
        args += [received[r] for r in ROUTES]
        in_specs += [hbm] * 4
        aliases[len(args)] = 0
        args.append(early[0])
        in_specs.append(hbm)
        if last:
            aliases[len(args)] = 1
            args += [early[1], early[2]]
            in_specs += [hbm, vmem]
    out_shape = [jax.ShapeDtypeStruct(lam.shape, lam.dtype)]
    out_specs = [hbm]
    if last:
        out_shape += [
            jax.ShapeDtypeStruct((owned, cells, width), jnp.float32),
            jax.ShapeDtypeStruct((devices if late else 1, width), jnp.float32),
        ]
        out_specs += [hbm, vmem]
    elif late:
        out_shape += [jax.ShapeDtypeStruct((2, rows, width), lam.dtype)] * 4
        out_specs += [hbm] * 4
    dma = pltpu.SemaphoreType.DMA
    return pl.pallas_call(
        functools.partial(step_kernel, late, last, step, devices),
        name=("late" if late else "early") + "_rows",
        out_shape=out_shape,
        in_specs=in_specs,
        out_specs=out_specs,
        input_output_aliases=aliases,
        scratch_shapes=[
            pltpu.VMEM((2 * owned + 1, rows, width), lam.dtype),
            pltpu.VMEM(ops.shape, ops.dtype),
            pltpu.VMEM(lam.shape, lam.dtype),
            pltpu.VMEM((owned, cells, width), jnp.float32),
            dma((5,)),
            dma((owned, ops.shape[1] // 2)),
            dma((owned,)),
            dma((owned,)),
            dma((4, 2)),
            pltpu.SMEM((owned,), jnp.int32),
        ],
        compiler_params=pltpu.CompilerParams(vmem_limit_bytes=40 * 1024 * 1024),
        cost_estimate=pl.CostEstimate(
            flops=2 * owned * 2 * rows * rows * width, bytes_accessed=8 << 20, transcendentals=0
        ),
    )(*args)


def scale_kernel(cells_total, sums, raw, out):
    meansq = jnp.sum(sums[...], axis=0, keepdims=True) / cells_total
    out[...] = raw[...] * lax.rsqrt(meansq + 1e-06)[None]


def scaled(sums, raw, cells_total):
    owned, cells, width = raw.shape
    return pl.pallas_call(
        functools.partial(scale_kernel, cells_total),
        name="scale",
        grid=(owned // 2,),
        out_shape=jax.ShapeDtypeStruct(raw.shape, raw.dtype),
        in_specs=[
            pl.BlockSpec(sums.shape, lambda i: (0, 0)),
            pl.BlockSpec((2, cells, width), lambda i: (i, 0, 0)),
        ],
        out_specs=pl.BlockSpec((2, cells, width), lambda i: (i, 0, 0)),
    )(sums, raw)


def per_device(
    adjoint_end,
    operator_blocks,
    block_cols,
    halo_send,
    wet_cells,
    gauge_cells,
    window_first,
    window_len,
    gauge_gain,
    snapshots,
):
    owned, cells = wet_cells.shape
    steps = snapshots.shape[0]
    devices = lax.axis_size("dom")
    halo = halo_send[0]
    factors = jnp.concatenate(
        [wet_cells.astype(jnp.float32)[:, None]]
        + [snapshots[t].reshape(owned, 3, cells) for t in range(steps)]
        + [jnp.zeros((owned, 1, cells), jnp.float32)],
        axis=1,
    )
    aux = jnp.swapaxes(factors, 1, 2)
    gauges = jnp.stack(
        [v.astype(jnp.float32) for v in (gauge_cells, window_first, window_len, gauge_gain)]
    )
    lam = adjoint_end
    sends = pick_sends(halo, lam)
    for step in range(steps):
        last = step == steps - 1
        common = (step, block_cols, halo, lam, operator_blocks, aux, gauges)
        received = exchange(sends)
        early = step_rows(False, last, *common)
        late = step_rows(True, last, *common, received=received, early=early)
        lam = late[0]
        if not last:
            sends = dict(zip(ROUTES, late[1:]))
    raw, squares = late[1:]
    sums = lax.all_to_all(squares, "dom", 0, 0, tiled=True)
    return (lam, scaled(sums, raw, devices * owned * cells))


def solution(mesh):
    return jax.shard_map(
        per_device,
        mesh=mesh,
        in_specs=(
            P("dom", None, None),
            P("dom", None, None, None),
            P("dom", None),
            P("dom", None, None),
            P("dom", None),
            P(),
            P(),
            P(),
            P(),
            P(None, "dom", None),
        ),
        out_specs=(P("dom", None, None), P("dom", None, None)),
        check_vma=False,
    )
```

time: 181 us -> 150 us (0.83)
  Pallas kernels: 0 us -> 76.4 us
  local copies, waits for them, and re-layouts: 65.3 us -> 6.2 us
  matrix products: 28.6 us -> 0 us
  blocking collectives: 44.8 us -> 20.5 us
  waiting for transfers between devices: 5.54 us -> 25.8 us
  other arithmetic: 9.13 us -> 1.72 us
  starting transfers between devices: 24.9 us -> 18.1 us
    pallas_call x0 -> x6, Pallas kernels: none -> 76.4 us  [the longest x1 49.5 us: pick_sends(): pl.pallas_call(pick_kernel, name='pick_sends', out_shape=[part] * 4, in_s...]
    gather x11 -> x0, local copies, waits for them, and re-layouts: 48.2 us -> none  [the longest x3 25.7 us: coupled_rows(): picked = extended[jnp.clip(block_cols, 0, last)]]
    psum x1 -> x0, blocking collectives: 44.8 us -> none  [per_device(): totals = lax.psum(jnp.sum(raw * raw, axis=(0, 1)), 'dom')]
    dot_general x2 -> x0, matrix products: 28.6 us -> none  [coupled_rows(): jnp.einsum('bkij,bkjf->bif', operator_blocks, picked, preferred_element_t...]
    all_to_all x0 -> x1, blocking collectives: none -> 20.5 us  [per_device(): sums = lax.all_to_all(squares, 'dom', 0, 0, tiled=True)]
    ppermute x8, waiting for transfers between devices: 5.54 us -> 25.8 us  [exchange(): lax.ppermute(sends[r], 'dom', pairs[r])]
    unnamed x43 -> x21, local copies, waits for them, and re-layouts: 9.34 us -> 1.64 us
    ppermute x8, starting transfers between devices: 24.9 us -> 18.1 us  [exchange(): lax.ppermute(sends[r], 'dom', pairs[r])]
  transfers between devices with their start and end apart: 8 -> 8, of which waited for: 2 -> 2; matrix products, arithmetic and copies ran while one was open for 17% -> 3% of each run, Pallas kernels for 0% -> 7%
where the time goes in v1:
time: 150 us
  Pallas kernels  76.4 us (51%)
  waiting for transfers between devices  25.8 us (17%)
  blocking collectives  20.5 us (14%)
  starting transfers between devices  18.1 us (12%)
  local copies, waits for them, and re-layouts  6.2 us (4%)
  other arithmetic  1.72 us (1%)
    pallas_call x1, Pallas kernels, pick_sends(): pl.pallas_call(pick_kernel, name='pick_sends', out_shape=[part] * 4, in_s...  49.5 us
    ppermute x8, waiting for transfers between devices, exchange(): lax.ppermute(sends[r], 'dom', pairs[r])  25.8 us
    pallas_call x4, Pallas kernels, step_rows(): pl.pallas_call(functools.partial(step_kernel, late, last, step, devices),...  23.4 us
    all_to_all x1, blocking collectives, per_device(): sums = lax.all_to_all(squares, 'dom', 0, 0, tiled=True)  20.5 us
    ppermute x8, starting transfers between devices, exchange(): lax.ppermute(sends[r], 'dom', pairs[r])  18.1 us
    pallas_call x1, Pallas kernels, scaled(): pl.pallas_call(functools.partial(scale_kernel, cells_total), name='scale'...  3.39 us
  transfers between devices with their start and end apart: 8, of which 2 were waited for; matrix products, arithmetic and copies ran while one was open for 3% of the time, Pallas kernels for 7%

profile of v1, /device:TPU:0, one launch (start us, length us, event | category | flops | bytes accessed | tf_op | source)
XLA Modules:
  0.0 149.6 jit_solution(18222250955882156865)
XLA Ops:
  0.6 0.0 copy-start.6
  0.7 1.4 copy.45.halo.refs_1_
  2.0 49.5 %pick_sends.1 = (bf16[2,384,256]{2,1,0:T(8,128)(2,1)}, bf16[2,384,256]{2,1,0:T(8,128)(2,1)}, bf16[2,384,256]{2,1,0:T(8,128)(2,1)}, bf16[2,384,256]{2,1,0:T(8,128)(2,1)}) custom-call(s32[4,2]{1,0:T(4,128)} %copy.45.halo.refs_1_, bf16[8,384,256]{2,1,0:T(8,128)(2,1)} %refs_2_.3), custom_call_target="tpu_custom_call" | custom-call | tf_op jit(solution)/shard_map/pick_sends/pallas_call | solution.py:53
  51.6 0.5 collective-permute-start
  52.1 0.7 collective-permute-start.1
  52.8 3.8 %collective-permute-start.2 = (bf16[2,384,256]{2,1,0:T(8,128)(2,1)}, bf16[2,384,256]{2,1,0:T(8,128)(2,1)S(1)}, u32[]{:S(2)}, u32[]{:S(2)}) collective-permute-start(bf16[2,384,256]{2,1,0:T(8,128)(2,1)} %get-tuple-element.19), channel_id=1, source_target_pairs={{0,2},{1,3},{2,0},{3,1},{4,6},{5,7},{6,4},{7,5},{8,10},{9,11},{10,... | collective-permute-start | bytes 1179656 | tf_op jit(solution)/shard_map/ppermute | solution.py:34
  56.6 0.7 collective-permute-start.3
  57.4 1.0 copy.39
  58.4 1.0 copy.38
  59.5 1.0 copy.40
  60.5 0.1 pad.7.clone
  60.6 1.7 %maximum_bitcast_fusion.refs_4_ = f32[8,128,8]{2,1,0:T(8,128)S(1)} fusion(f32[8,3,128]{1,2,0:T(8,128)} %copy.40, f32[8,3,128]{1,2,0:T(8,128)} %copy.39, f32[8,1,128]{1,2,0:T(8,128)} %copy.38, f32[8]{0:T(128)S(1)} %pad.7.clone), kind=kLoop, calls=%fused_computation | loop fusion | flops 24576 | bytes 61472 | tf_op jit(solution)/shard_map/transpose | solution.py:312
  62.3 4.9 %early_rows.2.refs_10_ = bf16[8,384,256]{2,1,0:T(8,128)(2,1)S(1)} custom-call(s32[8,6]{1,0:T(8,128)S(1)} %copy-done.3, s32[4,2]{1,0:T(4,128)S(1)} %copy-done.2, bf16[8,384,256]{2,1,0:T(8,128)(2,1)S(1)} %copy-done, bf16[8,6,384,384]{3,2,1,0:T(8,128)(2,1)} %refs_3_.7, f32[8,128,8]{2,1,0:T(8,128)S(1)} %maximum_bitcast_fusion.refs_4_, ...), custom_call_target="tpu_custom_call" | custom-call | flops 1207959552 | bytes 8388608 | tf_op jit(solution)/shard_map/early_rows/pallas_call | solution.py:244
  67.2 0.0 collective-permute-done.refs_6_
  67.2 0.0 collective-permute-done.1.refs_7_
  67.2 11.8 %collective-permute-done.2.refs_8_ = bf16[2,384,256]{2,1,0:T(8,128)(2,1)S(1)} collective-permute-done((bf16[2,384,256]{2,1,0:T(8,128)(2,1)}, bf16[2,384,256]{2,1,0:T(8,128)(2,1)S(1)}, u32[]{:S(2)}, u32[]{:S(2)}) %collective-permute-start.2) | collective-permute-done | bytes 393248 | tf_op jit(solution)/shard_map/ppermute | solution.py:34
  79.0 0.0 collective-permute-done.3.refs_9_
  79.0 7.6 %late_rows.2 = (bf16[8,384,256]{2,1,0:T(8,128)(2,1)S(1)}, bf16[2,384,256]{2,1,0:T(8,128)(2,1)S(1)}, bf16[2,384,256]{2,1,0:T(8,128)(2,1)S(1)}, bf16[2,384,256]{2,1,0:T(8,128)(2,1)S(1)}, bf16[2,384,256]{2,1,0:T(8,128)(2,1)S(1)}) custom-call(s32[8,6]{1,0:T(8,128)S(1)} %copy-done.3, s32[4,2]{1,0:T(4,128)S(1)} %copy-done.2, ...), custom_call_target="tpu_custom_call", output_to_operand_aliasing={{0}: (10, {})} | custom-call | flops 1207959552 | bytes 8388608 | tf_op jit(solution)/shard_map/late_rows/pallas_call | solution.py:244
  86.6 2.7 %collective-permute-start.4 = (bf16[2,384,256]{2,1,0:T(8,128)(2,1)S(1)}, bf16[2,384,256]{2,1,0:T(8,128)(2,1)S(1)}, u32[]{:S(2)}, u32[]{:S(2)}) collective-permute-start(bf16[2,384,256]{2,1,0:T(8,128)(2,1)S(1)} %get-tuple-element.22), channel_id=1, source_target_pairs={{0,1},{1,0},{2,3},{3,2},{4,5},{5,4},{6,7},{7,6},{8,9},{9,8},{10,11... | collective-permute-start | bytes 1179656 | tf_op jit(solution)/shard_map/ppermute | solution.py:34
  89.2 0.7 collective-permute-start.5
  89.9 8.4 %collective-permute-start.6 = (bf16[2,384,256]{2,1,0:T(8,128)(2,1)S(1)}, bf16[2,384,256]{2,1,0:T(8,128)(2,1)S(1)}, u32[]{:S(2)}, u32[]{:S(2)}) collective-permute-start(bf16[2,384,256]{2,1,0:T(8,128)(2,1)S(1)} %get-tuple-element.24), channel_id=1, source_target_pairs={{0,2},{1,3},{2,0},{3,1},{4,6},{5,7},{6,4},{7,5},{8,10},{9,11},{10,... | collective-permute-start | bytes 1179656 | tf_op jit(solution)/shard_map/ppermute | solution.py:34
  98.3 0.7 collective-permute-start.7
  99.0 5.2 %early_rows.3 = (bf16[8,384,256]{2,1,0:T(8,128)(2,1)}, f32[8,128,256]{2,1,0:T(8,128)S(1)}, f32[1,256]{1,0:T(1,128)S(1)}) custom-call(s32[8,6]{1,0:T(8,128)S(1)} %copy-done.3, s32[4,2]{1,0:T(4,128)S(1)} %copy-done.2, bf16[8,384,256]{2,1,0:T(8,128)(2,1)S(1)} %get-tuple-element.21.refs_2_, bf16[8,6,384,384]{3,2,1,0:T(8,128)(2,1)} %refs_3_.7, ...), custom_call_target="tpu_custom_call" | custom-call | flops 1207959552 | bytes 8388608 | tf_op jit(solution)/shard_map/early_rows/pallas_call | solution.py:244
  104.2 0.0 collective-permute-done.4.refs_6_
  104.2 0.0 collective-permute-done.5.refs_7_
  104.2 14.0 %collective-permute-done.6.refs_8_ = bf16[2,384,256]{2,1,0:T(8,128)(2,1)S(1)} collective-permute-done((bf16[2,384,256]{2,1,0:T(8,128)(2,1)S(1)}, bf16[2,384,256]{2,1,0:T(8,128)(2,1)S(1)}, u32[]{:S(2)}, u32[]{:S(2)}) %collective-permute-start.6) | collective-permute-done | bytes 393248 | tf_op jit(solution)/shard_map/ppermute | solution.py:34
  118.2 0.0 collective-permute-done.7.refs_9_
  118.2 5.8 %late_rows.3 = (bf16[8,384,256]{2,1,0:T(8,128)(2,1)}, f32[8,128,256]{2,1,0:T(8,128)S(1)}, f32[32,256]{1,0:T(8,128)S(1)}) custom-call(s32[8,6]{1,0:T(8,128)S(1)} %copy-done.3, s32[4,2]{1,0:T(4,128)S(1)} %copy-done.2, bf16[8,384,256]{2,1,0:T(8,128)(2,1)S(1)} %get-tuple-element.21.refs_2_, ...), custom_call_target="tpu_custom_call", output_to_operand_aliasing={{0}: (10, {}), {1}: (11, {})} | custom-call | flops 1207959552 | bytes 8388608 | tf_op jit(solution)/shard_map/late_rows/pallas_call | solution.py:244
  124.1 1.0 copy-done.1
  125.1 20.5 %all_to_all.11 = f32[32,1,256]{2,1,0:T(1,128)S(1)} all-to-all(f32[32,1,256]{2,1,0:T(1,128)S(1)} %copy.46), channel_id=1, replica_groups=mesh['dom'=32] {'dom'}, dimensions={0} | all-to-all | bytes 65536 | tf_op jit(solution)/shard_map/all_to_all | solution.py:328
  145.6 0.6 copy.49
  146.2 3.4 %scale.1 = f32[8,128,256]{2,1,0:T(8,128)} custom-call(f32[32,256]{1,0:T(8,128)} %bitcast.19, f32[8,128,256]{2,1,0:T(8,128)} %copy-done.1), custom_call_target="tpu_custom_call" | custom-call | tf_op jit(solution)/shard_map/scale/pallas_call | solution.py:277
  (25 shorter events, 0.1 us)
Async XLA Ops:
  0.6 56.6 %copy-start.6 = (s32[256]{0:T(256)S(1)}, s32[256]{0:T(256)}, u32[]{:S(2)}) copy-start(s32[256]{0:T(256)} %param.15) | copy-start | bytes 3076
  0.6 56.7 %copy-start.7 = (s32[256]{0:T(256)S(1)}, s32[256]{0:T(256)}, u32[]{:S(2)}) copy-start(s32[256]{0:T(256)} %param.16) | copy-start | bytes 3076
  0.7 56.7 %copy-start.8 = (s32[256]{0:T(256)S(1)}, s32[256]{0:T(256)}, u32[]{:S(2)}) copy-start(s32[256]{0:T(256)} %param.17) | copy-start | bytes 3076
  0.7 56.7 %copy-start.5 = (s32[8,128]{1,0:T(8,128)S(1)}, s32[8,128]{1,0:T(8,128)}, u32[]{:S(2)}) copy-start(s32[8,128]{1,0:T(8,128)} %param.14) | copy-start | bytes 12292
  0.7 56.7 %copy-start.4 = (f32[2,8,384]{2,1,0:T(8,128)S(1)}, f32[2,8,384]{2,1,0:T(8,128)}, u32[]{:S(2)}) copy-start(f32[2,8,384]{2,1,0:T(8,128)} %param.19) | copy-start | bytes 73732
  0.7 56.7 %copy-start.9 = (f32[256]{0:T(256)S(1)}, f32[256]{0:T(256)}, u32[]{:S(2)}) copy-start(f32[256]{0:T(256)} %param.18) | copy-start | bytes 3076
  51.6 15.6 %collective-permute-start = (bf16[2,384,256]{2,1,0:T(8,128)(2,1)}, bf16[2,384,256]{2,1,0:T(8,128)(2,1)S(1)}, u32[]{:S(2)}, u32[]{:S(2)}) collective-permute-start(bf16[2,384,256]{2,1,0:T(8,128)(2,1)} %get-tuple-element.17), channel_id=1, source_target_pairs={{0,1},{1,0},{2,3},{3,2},{4,5},{5,4},{6,7},{7,6},{8,9},{9,8},{10,11... | collective-permute-start | bytes 1179656 | tf_op jit(solution)/shard_map/ppermute | solution.py:34
  52.1 15.1 %collective-permute-start.1 = (bf16[2,384,256]{2,1,0:T(8,128)(2,1)}, bf16[2,384,256]{2,1,0:T(8,128)(2,1)S(1)}, u32[]{:S(2)}, u32[]{:S(2)}) collective-permute-start(bf16[2,384,256]{2,1,0:T(8,128)(2,1)} %get-tuple-element.18), channel_id=1, source_target_pairs={{1,2},{3,4},{5,6},{7,8},{9,10},{11,12},{13,14},{15,16},{17,18},{19... | collective-permute-start | bytes 1179656 | tf_op jit(solution)/shard_map/ppermute | solution.py:34
  52.8 26.2 %collective-permute-start.2 = (bf16[2,384,256]{2,1,0:T(8,128)(2,1)}, bf16[2,384,256]{2,1,0:T(8,128)(2,1)S(1)}, u32[]{:S(2)}, u32[]{:S(2)}) collective-permute-start(bf16[2,384,256]{2,1,0:T(8,128)(2,1)} %get-tuple-element.19), channel_id=1, source_target_pairs={{0,2},{1,3},{2,0},{3,1},{4,6},{5,7},{6,4},{7,5},{8,10},{9,11},{10,... | collective-permute-start | bytes 1179656 | tf_op jit(solution)/shard_map/ppermute | solution.py:34
  56.6 22.4 %collective-permute-start.3 = (bf16[2,384,256]{2,1,0:T(8,128)(2,1)}, bf16[2,384,256]{2,1,0:T(8,128)(2,1)S(1)}, u32[]{:S(2)}, u32[]{:S(2)}) collective-permute-start(bf16[2,384,256]{2,1,0:T(8,128)(2,1)} %get-tuple-element.20), channel_id=1, source_target_pairs={{2,4},{3,5},{6,8},{7,9},{10,12},{11,13},{14,16},{15,17},{18,20},{1... | collective-permute-start | bytes 1179656 | tf_op jit(solution)/shard_map/ppermute | solution.py:34
  58.4 3.8 %copy-start = (bf16[8,384,256]{2,1,0:T(8,128)(2,1)S(1)}, bf16[8,384,256]{2,1,0:T(8,128)(2,1)}, u32[]{:S(2)}) copy-start(bf16[8,384,256]{2,1,0:T(8,128)(2,1)} %refs_2_.3) | copy-start | bytes 4718596
  58.4 3.9 %copy-start.2 = (s32[4,2]{1,0:T(4,128)S(1)}, s32[4,2]{1,0:T(4,128)}, u32[]{:S(2)}) copy-start(s32[4,2]{1,0:T(4,128)} %copy.45.halo.refs_1_) | copy-start | bytes 100
  58.4 3.9 %copy-start.3 = (s32[8,6]{1,0:T(8,128)S(1)}, s32[8,6]{1,0:T(8,128)}, u32[]{:S(2)}) copy-start(s32[8,6]{1,0:T(8,128)} %refs_0_.7) | copy-start | bytes 580
  86.6 17.6 %collective-permute-start.4 = (bf16[2,384,256]{2,1,0:T(8,128)(2,1)S(1)}, bf16[2,384,256]{2,1,0:T(8,128)(2,1)S(1)}, u32[]{:S(2)}, u32[]{:S(2)}) collective-permute-start(bf16[2,384,256]{2,1,0:T(8,128)(2,1)S(1)} %get-tuple-element.22), channel_id=1, source_target_pairs={{0,1},{1,0},{2,3},{3,2},{4,5},{5,4},{6,7},{7,6},{8,9},{9,8},{10,11... | collective-permute-start | bytes 1179656 | tf_op jit(solution)/shard_map/ppermute | solution.py:34
  89.2 14.9 %collective-permute-start.5 = (bf16[2,384,256]{2,1,0:T(8,128)(2,1)S(1)}, bf16[2,384,256]{2,1,0:T(8,128)(2,1)S(1)}, u32[]{:S(2)}, u32[]{:S(2)}) collective-permute-start(bf16[2,384,256]{2,1,0:T(8,128)(2,1)S(1)} %get-tuple-element.23), channel_id=1, source_target_pairs={{1,2},{3,4},{5,6},{7,8},{9,10},{11,12},{13,14},{15,16},{17,18},{19... | collective-permute-start | bytes 1179656 | tf_op jit(solution)/shard_map/ppermute | solution.py:34
  89.9 28.3 %collective-permute-start.6 = (bf16[2,384,256]{2,1,0:T(8,128)(2,1)S(1)}, bf16[2,384,256]{2,1,0:T(8,128)(2,1)S(1)}, u32[]{:S(2)}, u32[]{:S(2)}) collective-permute-start(bf16[2,384,256]{2,1,0:T(8,128)(2,1)S(1)} %get-tuple-element.24), channel_id=1, source_target_pairs={{0,2},{1,3},{2,0},{3,1},{4,6},{5,7},{6,4},{7,5},{8,10},{9,11},{10,... | collective-permute-start | bytes 1179656 | tf_op jit(solution)/shard_map/ppermute | solution.py:34
  98.3 19.9 %collective-permute-start.7 = (bf16[2,384,256]{2,1,0:T(8,128)(2,1)S(1)}, bf16[2,384,256]{2,1,0:T(8,128)(2,1)S(1)}, u32[]{:S(2)}, u32[]{:S(2)}) collective-permute-start(bf16[2,384,256]{2,1,0:T(8,128)(2,1)S(1)} %get-tuple-element.25), channel_id=1, source_target_pairs={{2,4},{3,5},{6,8},{7,9},{10,12},{11,13},{14,16},{15,17},{18,20},{1... | collective-permute-start | bytes 1179656 | tf_op jit(solution)/shard_map/ppermute | solution.py:34
  124.0 1.0 copy-start.1

commit v2 on v1

v2 whole, which is shorter than its diff:
```python
import functools

import jax
import jax.numpy as jnp
from jax import lax
from jax.experimental import pallas as pl
from jax.experimental.pallas import tpu as pltpu
from jax.sharding import PartitionSpec as P

ROUTES = ("swap", "cross", "inner", "outer")


def route_pairs(devices):
    swap = [(i, i ^ 1) for i in range(devices)]
    cross = [(i, i + 1) for i in range(1, devices - 1, 2)]
    inner = [(i, i ^ 2) for i in range(devices)]
    outer = [(i, i + 2) for i in range(devices - 2) if i & 2]
    both = lambda pairs: pairs + [(j, i) for i, j in pairs]
    return dict(swap=swap, cross=both(cross), inner=inner, outer=both(outer))


def send_groups(device):
    core, chip = device % 2, (device // 2) % 2
    return dict(swap=2 - core, cross=1 + core, inner=3 - 3 * chip, outer=3 * chip)


def receive_groups(device):
    core, chip = device % 2, (device // 2) % 2
    return dict(swap=1 + core, cross=2 - core, inner=3 * chip, outer=3 - 3 * chip)


def exchange(sends):
    pairs = route_pairs(lax.axis_size("dom"))
    return {r: lax.ppermute(sends[r], "dom", pairs[r]) for r in ("inner", "cross", "outer", "swap")}


def pinned(value):
    return pltpu.with_memory_space_constraint(value, pltpu.VMEM)


def pick_kernel(halo, lam, *rest):
    outs, sems = dict(zip(ROUTES, rest[:4])), rest[4]
    groups = send_groups(lax.axis_index("dom"))
    copies = []
    for i, r in enumerate(ROUTES):
        for c in range(2):
            row = jnp.maximum(halo[0, groups[r], c], 0)
            copies.append(pltpu.make_async_copy(lam.at[row], outs[r].at[c], sems.at[i, c]))
    for copy in copies:
        copy.start()
    for copy in copies:
        copy.wait()


def pick_sends(halo, lam):
    part = pltpu.VMEM((2,) + lam.shape[1:], lam.dtype)
    outs = pl.pallas_call(
        pick_kernel,
        name="pick_sends",
        out_shape=[part] * 4,
        in_specs=[pl.BlockSpec(memory_space=pltpu.SMEM), pl.BlockSpec(memory_space=pltpu.HBM)],
        out_specs=[pl.BlockSpec(memory_space=pltpu.VMEM)] * 4,
        scratch_shapes=[pltpu.SemaphoreType.DMA((4, 2))],
    )(halo, lam)
    return dict(zip(ROUTES, outs))


def step_kernel(late, last, step, *refs):
    refs = list(refs)
    take = lambda n: [refs.pop(0) for _ in range(n)]
    cols, halo, lam, ops, aux, gauges = take(6)
    received = take(4) if late else []
    take(1 + last if late else 0)
    done_squares = take(1)[0] if late and last else None
    (new,) = take(1)
    raw, squares = take(2) if last else (None, None)
    sends = dict(zip(ROUTES, take(4))) if late and not last else {}
    (slots,) = refs if late else (None,)

    owned, entries = ops.shape[0], ops.shape[1]
    rows, width = lam.shape[1], lam.shape[2]
    cells = rows // 3
    position = lax.axis_index("dom")

    if late:
        groups = receive_groups(position)
        for i, r in enumerate(ROUTES):
            slots[pl.ds(2 * groups[r], 2)] = received[i][...]
    if last:
        if late:
            squares[...] = jnp.broadcast_to(done_squares[...], squares.shape)
        else:
            squares[...] = jnp.zeros(squares.shape, jnp.float32)

    first = gauges[1:2, :]
    active = jnp.where(
        jnp.logical_and(first <= step, step < first + gauges[2:3, :]), gauges[3:4, :], 0.0
    )
    own_cells = lax.broadcasted_iota(jnp.int32, (cells, width), 0)

    def finish(b, total):
        wet = aux[b, :, 0:1]
        where = gauges[0:1, :].astype(jnp.int32) - (position * owned + b) * cells
        source = jnp.where(own_cells == where, active, 0.0)
        gathered = None
        for c in range(3):
            part = pl.ds(c * cells, cells)
            before = lam[b, part, :].astype(jnp.float32)
            updated = wet * (before + total[c * cells : (c + 1) * cells])
            if c == 0:
                updated = updated + source
            updated = updated.astype(jnp.bfloat16)
            new[b, part, :] = updated
            if last:
                term = aux[b, :, 1 + c : 2 + c] * before
                gathered = term if gathered is None else gathered + term
                gathered = gathered + aux[b, :, 4 + c : 5 + c] * updated.astype(jnp.float32)
        if last:
            raw[b] = gathered
            squares[...] += jnp.broadcast_to(
                jnp.sum(gathered * gathered, axis=0, keepdims=True)[None], squares.shape
            )

    def picked(b, k):
        col = cols[b, k]
        block = lam[jnp.clip(col, 0, owned - 1)]
        if late:
            block = jnp.where(col < owned, block, slots[jnp.maximum(col - owned, 0)])
        return jnp.where(col >= 0, block, jnp.zeros_like(block))

    def make_row(b, n):
        state = [lam[b]] + [picked(b, k) for k in range(1, 2 * n)]
        weights = jnp.concatenate([ops[b, k] for k in range(2 * n)], axis=1)
        total = jnp.dot(
            weights, jnp.concatenate(state, axis=0), preferred_element_type=jnp.float32
        )
        finish(b, total)

    def shape_of(b):
        live, top = 0, -1
        for k in range(entries):
            live = live + (cols[b, k] >= 0).astype(jnp.int32)
            top = jnp.maximum(top, cols[b, k])
        return (live + 1) // 2, (top >= owned) if late else (top < owned)

    def each_row():
        @pl.loop(0, owned)
        def _(b):
            pairs, mine = shape_of(b)
            for n in range(1, entries // 2 + 1):

                @pl.when(jnp.logical_and(mine, pairs == n))
                def _(n=n):
                    make_row(b, n)

    if late:
        plain = True
        for b in range(owned):
            pairs, mine = shape_of(b)
            plain = jnp.logical_and(plain, jnp.logical_and(mine, pairs == 1))

        @pl.when(plain)
        def _():
            for b in range(owned):
                make_row(b, 1)

        @pl.when(jnp.logical_not(plain))
        def _():
            each_row()
    else:
        each_row()

    if sends:
        groups = send_groups(position)
        for r in ROUTES:
            for c in range(2):
                sends[r][c] = new[jnp.maximum(halo[0, groups[r], c], 0)]


def step_rows(late, last, step, cols, halo, lam, ops, aux, gauges, received=None, early=None):
    owned, rows, width = lam.shape
    cells = rows // 3
    devices = lax.axis_size("dom")
    smem, vmem = (pl.BlockSpec(memory_space=m) for m in (pltpu.SMEM, pltpu.VMEM))
    args = [cols, halo, pinned(lam), pinned(ops), aux, gauges]
    aliases = {}
    if late:
        args += [pinned(received[r]) for r in ROUTES]
        for i in range(1 + last):
            aliases[len(args)] = i
            args.append(pinned(early[i]))
        if last:
            args.append(early[2])
    out_shape = [pltpu.VMEM(lam.shape, lam.dtype)]
    if last:
        out_shape += [
            pltpu.VMEM((owned, cells, width), jnp.float32),
            pltpu.VMEM((devices if late else 1, 1, width), jnp.float32),
        ]
    elif late:
        out_shape += [pltpu.VMEM((2, rows, width), lam.dtype)] * 4
    return pl.pallas_call(
        functools.partial(step_kernel, late, last, step),
        name=("late" if late else "early") + "_rows",
        out_shape=out_shape,
        in_specs=[smem, smem] + [vmem] * (len(args) - 2),
        out_specs=[vmem] * len(out_shape),
        input_output_aliases=aliases,
        scratch_shapes=[pltpu.VMEM((owned, rows, width), lam.dtype)] if late else [],
        compiler_params=pltpu.CompilerParams(vmem_limit_bytes=16 * 1024 * 1024),
        cost_estimate=pl.CostEstimate(
            flops=2 * owned * 2 * rows * rows * width, bytes_accessed=8 << 20, transcendentals=0
        ),
    )(*args)


def scale_kernel(cells_total, sums, raw, out, scaled_rows, sems):
    factor = lax.rsqrt(jnp.sum(sums[...], axis=0) / cells_total + 1e-06)
    copies = []
    for b in range(raw.shape[0]):
        scaled_rows[b] = raw[b] * factor
        copies.append(pltpu.make_async_copy(scaled_rows.at[b], out.at[b], sems.at[b]))
        copies[b].start()
    for copy in copies:
        copy.wait()


def scaled(sums, raw, cells_total):
    vmem = pl.BlockSpec(memory_space=pltpu.VMEM)
    return pl.pallas_call(
        functools.partial(scale_kernel, cells_total),
        name="scale",
        out_shape=jax.ShapeDtypeStruct(raw.shape, raw.dtype),
        in_specs=[vmem, vmem],
        out_specs=pl.BlockSpec(memory_space=pltpu.HBM),
        scratch_shapes=[
            pltpu.VMEM(raw.shape, raw.dtype),
            pltpu.SemaphoreType.DMA((raw.shape[0],)),
        ],
    )(sums, pinned(raw))


def per_device(
    adjoint_end,
    operator_blocks,
    block_cols,
    halo_send,
    wet_cells,
    gauge_cells,
    window_first,
    window_len,
    gauge_gain,
    snapshots,
):
    owned, cells = wet_cells.shape
    steps = snapshots.shape[0]
    devices = lax.axis_size("dom")
    factors = jnp.concatenate(
        [wet_cells.astype(jnp.float32)[:, None]]
        + [snapshots[t].reshape(owned, 3, cells) for t in range(steps)]
        + [jnp.zeros((owned, 1, cells), jnp.float32)],
        axis=1,
    )
    aux = jnp.swapaxes(factors, 1, 2)
    gauges = jnp.stack(
        [v.astype(jnp.float32) for v in (gauge_cells, window_first, window_len, gauge_gain)]
    )
    lam = adjoint_end
    sends = pick_sends(halo_send, lam)
    for step in range(steps):
        last = step == steps - 1
        common = (step, block_cols, halo_send, lam, operator_blocks, aux, gauges)
        received = exchange(sends)
        early = step_rows(False, last, *common)
        late = step_rows(True, last, *common, received=received, early=early)
        lam = late[0]
        if not last:
            sends = dict(zip(ROUTES, late[1:]))
    raw, squares = late[1:]
    sums = lax.all_to_all(squares, "dom", 0, 0, tiled=True)
    return (lam, scaled(sums, raw, devices * owned * cells))


def solution(mesh):
    return jax.shard_map(
        per_device,
        mesh=mesh,
        in_specs=(
            P("dom", None, None),
            P("dom", None, None, None),
            P("dom", None),
            P("dom", None, None),
            P("dom", None),
            P(),
            P(),
            P(),
            P(),
            P(None, "dom", None),
        ),
        out_specs=(P("dom", None, None), P("dom", None, None)),
        check_vma=False,
    )
```

time: 150 us -> 89.6 us (0.60)
  Pallas kernels: 76.4 us -> 15.9 us
  blocking collectives: 20.5 us -> 0 us
  starting transfers between devices: 18.1 us -> 27 us
  local copies, waits for them, and re-layouts: 6.2 us -> 12.7 us
  waiting for transfers between devices: 25.8 us -> 30.8 us
    pallas_call x1, Pallas kernels: 49.5 us -> 3.39 us  [pick_sends(): pl.pallas_call(pick_kernel, name='pick_sends', out_shape=[part] * 4, in_s...]
    all_to_all x1 -> x0, blocking collectives: 20.5 us -> none  [per_device(): sums = lax.all_to_all(squares, 'dom', 0, 0, tiled=True)]
    pallas_call x4, Pallas kernels: 23.4 us -> 10.7 us  [step_rows(): pl.pallas_call(functools.partial(step_kernel, late, last, step), name=('l...]
    all_to_all x0 -> x1, starting transfers between devices: none -> 11.8 us  [per_device(): sums = lax.all_to_all(squares, 'dom', 0, 0, tiled=True)]
    unnamed x21 -> x32, local copies, waits for them, and re-layouts: 1.64 us -> 8.21 us
    all_to_all x0 -> x1, waiting for transfers between devices: none -> 6.1 us  [per_device(): sums = lax.all_to_all(squares, 'dom', 0, 0, tiled=True)]
    ppermute x8, starting transfers between devices: 18.1 us -> 15.2 us  [exchange(): lax.ppermute(sends[r], 'dom', pairs[r])]
    pallas_call x1, Pallas kernels: 3.39 us -> 1.84 us  [scaled(): pl.pallas_call(functools.partial(scale_kernel, cells_total), name='scale'...]
  transfers between devices with their start and end apart: 8 -> 9, of which waited for: 2 -> 3; matrix products, arithmetic and copies ran while one was open for 3% -> 8% of each run, Pallas kernels for 7% -> 5%
where the time goes in v2:
time: 89.6 us; the launch traced here: 89.1 us
  waiting for transfers between devices  30.8 us (34%)
  starting transfers between devices  27 us (30%)
  Pallas kernels  15.9 us (18%)
  local copies, waits for them, and re-layouts  12.7 us (14%)
  other arithmetic  1.72 us (2%)
  between operations  0.96 us (1%)
    ppermute x8, waiting for transfers between devices, exchange(): lax.ppermute(sends[r], 'dom', pairs[r])  24.7 us
    ppermute x8, starting transfers between devices, exchange(): lax.ppermute(sends[r], 'dom', pairs[r])  15.2 us
    all_to_all x1, starting transfers between devices, per_device(): sums = lax.all_to_all(squares, 'dom', 0, 0, tiled=True)  11.8 us
    pallas_call x4, Pallas kernels, step_rows(): pl.pallas_call(functools.partial(step_kernel, late, last, step), name=('l...  10.7 us
    unnamed x32, local copies, waits for them, and re-layouts  8.21 us
    all_to_all x1, waiting for transfers between devices, per_device(): sums = lax.all_to_all(squares, 'dom', 0, 0, tiled=True)  6.1 us
    pallas_call x1, Pallas kernels, pick_sends(): pl.pallas_call(pick_kernel, name='pick_sends', out_shape=[part] * 4, in_s...  3.39 us
    another operation x3, local copies, waits for them, and re-layouts, per_device(): snapshots[t].reshape(owned, 3, cells)  3.35 us
  transfers between devices with their start and end apart: 9, of which 3 were waited for; matrix products, arithmetic and copies ran while one was open for 8% of the time, Pallas kernels for 5%

profile of v2, /device:TPU:0, one launch (start us, length us, event | category | flops | bytes accessed | tf_op | source)
XLA Modules:
  0.0 89.1 jit_solution(3703116112745855336)
XLA Ops:
  0.7 1.4 %copy.44.halo.refs_1_ = s32[1,4,2]{2,1,0:T(4,128)} copy(s32[1,4,2]{1,2,0:T(2,128)} %param.13) | data formatting | bytes 64 | tf_op args[3]
  2.1 3.4 %pick_sends.1 = (bf16[2,384,256]{2,1,0:T(8,128)(2,1)}, bf16[2,384,256]{2,1,0:T(8,128)(2,1)}, bf16[2,384,256]{2,1,0:T(8,128)(2,1)}, bf16[2,384,256]{2,1,0:T(8,128)(2,1)S(1)}) custom-call(s32[1,4,2]{2,1,0:T(4,128)} %copy.44.halo.refs_1_, bf16[8,384,256]{2,1,0:T(8,128)(2,1)} %refs_2_.3), custom_call_target="tpu_custom_call" | custom-call | tf_op jit(solution)/shard_map/pick_sends/pallas_call | solution.py:57
  5.5 0.4 collective-permute-start
  5.9 0.7 collective-permute-start.1
  6.6 3.8 %collective-permute-start.2 = (bf16[2,384,256]{2,1,0:T(8,128)(2,1)}, bf16[2,384,256]{2,1,0:T(8,128)(2,1)S(1)}, u32[]{:S(2)}, u32[]{:S(2)}) collective-permute-start(bf16[2,384,256]{2,1,0:T(8,128)(2,1)} %get-tuple-element.19), channel_id=1, source_target_pairs={{0,2},{1,3},{2,0},{3,1},{4,6},{5,7},{6,4},{7,5},{8,10},{9,11},{10,... | collective-permute-start | bytes 1179656 | tf_op jit(solution)/shard_map/ppermute | solution.py:34
  10.4 0.7 collective-permute-start.3
  11.2 0.6 slice_bitcast_fusion.1
  11.8 1.0 %copy.38 = f32[8,3,128]{1,2,0:T(8,128)} copy(f32[8,3,128]{2,0,1:T(8,128)S(1)} %get-tuple-element.32) | data formatting | bytes 24576 | tf_op jit(solution)/shard_map/reshape;squeeze | solution.py:260
  12.8 1.0 %copy.37 = f32[8,1,128]{1,2,0:T(8,128)} copy(f32[8,1,128]{2,0,1:T(8,128)S(1)} %convert_bitcast_fusion) | data formatting | bytes 8192 | tf_op jit(solution)/shard_map/broadcast_in_dim | solution.py:259
  13.8 1.7 %copy.39 = f32[8,3,128]{1,2,0:T(8,128)} copy(f32[8,3,128]{2,0,1:T(8,128)} %get-tuple-element.33) | data formatting | bytes 24576 | tf_op jit(solution)/shard_map/reshape;squeeze | solution.py:260
  15.6 0.1 pad.7.clone
  15.6 1.7 %maximum_bitcast_fusion.refs_4_ = f32[8,128,8]{2,1,0:T(8,128)S(1)} fusion(f32[8,3,128]{1,2,0:T(8,128)} %copy.39, f32[8,3,128]{1,2,0:T(8,128)} %copy.38, f32[8,1,128]{1,2,0:T(8,128)} %copy.37, f32[8]{0:T(128)S(1)} %pad.7.clone), kind=kLoop, calls=%fused_computation | loop fusion | flops 24576 | bytes 61472 | tf_op jit(solution)/shard_map/transpose | solution.py:264
  17.4 0.0 copy-start
  17.4 5.0 %copy-done = bf16[8,6,384,384]{3,2,1,0:T(8,128)(2,1)S(1)} copy-done((bf16[8,6,384,384]{3,2,1,0:T(8,128)(2,1)S(1)}, bf16[8,6,384,384]{3,2,1,0:T(8,128)(2,1)}, u32[]{:S(2)}) %copy-start) | copy-done | bytes 14155800
  22.4 2.3 %early_rows.2.refs_10_ = bf16[8,384,256]{2,1,0:T(8,128)(2,1)S(1)} custom-call(s32[8,6]{1,0:T(8,128)S(1)} %copy-done.3, s32[1,4,2]{2,1,0:T(4,128)S(1)} %copy-done.2, bf16[8,384,256]{2,1,0:T(8,128)(2,1)S(1)} %copy-done.1, bf16[8,6,384,384]{3,2,1,0:T(8,128)(2,1)S(1)} %copy-done, f32[8,128,8]{2,1,0:T(8,128)S(1)} %maximum_bitcast_fusion.refs_4_, ...), custom_call_target="tpu_custom_call" | custom-call | flops 1207959552 | bytes 8388608 | tf_op jit(solution)/shard_map/early_rows/pallas_call | solution.py:202
  24.7 0.0 slice-start.2
  24.7 0.0 slice-start.3
  24.7 0.0 collective-permute-done.refs_6_
  24.7 8.1 %collective-permute-done.2.refs_8_ = bf16[2,384,256]{2,1,0:T(8,128)(2,1)S(1)} collective-permute-done((bf16[2,384,256]{2,1,0:T(8,128)(2,1)}, bf16[2,384,256]{2,1,0:T(8,128)(2,1)S(1)}, u32[]{:S(2)}, u32[]{:S(2)}) %collective-permute-start.2) | collective-permute-done | bytes 393248 | tf_op jit(solution)/shard_map/ppermute | solution.py:34
  32.8 2.5 %late_rows.2 = (bf16[8,384,256]{2,1,0:T(8,128)(2,1)S(1)}, bf16[2,384,256]{2,1,0:T(8,128)(2,1)S(1)}, bf16[2,384,256]{2,1,0:T(8,128)(2,1)S(1)}, bf16[2,384,256]{2,1,0:T(8,128)(2,1)S(1)}, bf16[2,384,256]{2,1,0:T(8,128)(2,1)S(1)}) custom-call(s32[8,6]{1,0:T(8,128)S(1)} %copy-done.3, s32[1,4,2]{2,1,0:T(4,128)S(1)} %copy-done.2, ...), custom_call_target="tpu_custom_call", output_to_operand_aliasing={{0}: (10, {})} | custom-call | flops 1207959552 | bytes 8388608 | tf_op jit(solution)/shard_map/late_rows/pallas_call | solution.py:202
  35.3 3.8 %collective-permute-start.4 = (bf16[2,384,256]{2,1,0:T(8,128)(2,1)S(1)}, bf16[2,384,256]{2,1,0:T(8,128)(2,1)S(1)}, u32[]{:S(2)}, u32[]{:S(2)}) collective-permute-start(bf16[2,384,256]{2,1,0:T(8,128)(2,1)S(1)} %get-tuple-element.22), channel_id=1, source_target_pairs={{0,1},{1,0},{2,3},{3,2},{4,5},{5,4},{6,7},{7,6},{8,9},{9,8},{10,11... | collective-permute-start | bytes 1179656 | tf_op jit(solution)/shard_map/ppermute | solution.py:34
  39.1 0.7 collective-permute-start.5
  39.8 4.5 %collective-permute-start.6 = (bf16[2,384,256]{2,1,0:T(8,128)(2,1)S(1)}, bf16[2,384,256]{2,1,0:T(8,128)(2,1)S(1)}, u32[]{:S(2)}, u32[]{:S(2)}) collective-permute-start(bf16[2,384,256]{2,1,0:T(8,128)(2,1)S(1)} %get-tuple-element.24), channel_id=1, source_target_pairs={{0,2},{1,3},{2,0},{3,1},{4,6},{5,7},{6,4},{7,5},{8,10},{9,11},{10,... | collective-permute-start | bytes 1179656 | tf_op jit(solution)/shard_map/ppermute | solution.py:34
  44.3 0.7 collective-permute-start.7
  45.0 2.5 %early_rows.3 = (bf16[8,384,256]{2,1,0:T(8,128)(2,1)S(1)}, f32[8,128,256]{2,1,0:T(8,128)S(1)}, f32[1,1,256]{2,1,0:T(1,128)S(1)}) custom-call(s32[8,6]{1,0:T(8,128)S(1)} %copy-done.3, s32[1,4,2]{2,1,0:T(4,128)S(1)} %copy-done.2, bf16[8,384,256]{2,1,0:T(8,128)(2,1)S(1)} %get-tuple-element.21.refs_2_, bf16[8,6,384,384]{3,2,1,0:T(8,128)(2,1)S(1)} %bitcast.14, ...), custom_call_target="tpu_custom_call" | custom-call | flops 1207959552 | bytes 8388608 | tf_op jit(solution)/shard_map/early_rows/pallas_call | solution.py:202
  47.6 16.6 %collective-permute-done.6.refs_8_ = bf16[2,384,256]{2,1,0:T(8,128)(2,1)S(1)} collective-permute-done((bf16[2,384,256]{2,1,0:T(8,128)(2,1)S(1)}, bf16[2,384,256]{2,1,0:T(8,128)(2,1)S(1)}, u32[]{:S(2)}, u32[]{:S(2)}) %collective-permute-start.6) | collective-permute-done | bytes 393248 | tf_op jit(solution)/shard_map/ppermute | solution.py:34
  64.2 3.4 %late_rows.3 = (bf16[8,384,256]{2,1,0:T(8,128)(2,1)S(1)}, f32[8,128,256]{2,1,0:T(8,128)S(1)}, f32[32,1,256]{2,1,0:T(1,128)}) custom-call(s32[8,6]{1,0:T(8,128)S(1)} %copy-done.3, s32[1,4,2]{2,1,0:T(4,128)S(1)} %copy-done.2, bf16[8,384,256]{2,1,0:T(8,128)(2,1)S(1)} %get-tuple-element.21.refs_2_, ...), custom_call_target="tpu_custom_call", output_to_operand_aliasing={{0}: (10, {}), {1}: (11, {})} | custom-call | flops 1207959552 | bytes 8388608 | tf_op jit(solution)/shard_map/late_rows/pallas_call | solution.py:202
  67.6 11.8 %all-to-all-start = ((f32[32,1,256]{2,1,0:T(1,128)}), f32[32,1,256]{2,1,0:T(1,128)S(1)}, u32[]{:S(2)}, u32[]{:S(2)}) async-start(f32[32,1,256]{2,1,0:T(1,128)} %get-tuple-element.30), calls=%async_computation | async-start | bytes 65536 | tf_op jit(solution)/shard_map/all_to_all | solution.py:280
  79.4 1.1 %copy.48 = bf16[8,384,256]{2,1,0:T(8,128)(2,1)} copy(bf16[8,384,256]{2,1,0:T(8,128)(2,1)S(1)} %get-tuple-element.34) | data formatting | bytes 3145728
  80.5 6.1 %all-to-all-done.sums = f32[32,1,256]{2,1,0:T(1,128)S(1)} async-done(((f32[32,1,256]{2,1,0:T(1,128)}), f32[32,1,256]{2,1,0:T(1,128)S(1)}, u32[]{:S(2)}, u32[]{:S(2)}) %all-to-all-start) | async-done | bytes 32800 | tf_op jit(solution)/shard_map/all_to_all | solution.py:280
  86.6 0.6 copy-done.4
  87.3 1.8 %scale.1 = f32[8,128,256]{2,1,0:T(8,128)} custom-call(f32[32,1,256]{2,1,0:T(1,128)} %copy-done.4, f32[8,128,256]{2,1,0:T(8,128)S(1)} %get-tuple-element.31.raw), custom_call_target="tpu_custom_call" | custom-call | tf_op jit(solution)/shard_map/scale/pallas_call | solution.py:230
  (36 shorter events, 0.1 us)
Async XLA Ops:
  0.6 10.4 %copy-start.7 = (s32[256]{0:T(256)S(1)}, s32[256]{0:T(256)}, u32[]{:S(2)}) copy-start(s32[256]{0:T(256)} %param.15) | copy-start | bytes 3076
  0.6 10.4 %copy-start.8 = (s32[256]{0:T(256)S(1)}, s32[256]{0:T(256)}, u32[]{:S(2)}) copy-start(s32[256]{0:T(256)} %param.16) | copy-start | bytes 3076
  0.7 10.5 %copy-start.9 = (s32[256]{0:T(256)S(1)}, s32[256]{0:T(256)}, u32[]{:S(2)}) copy-start(s32[256]{0:T(256)} %param.17) | copy-start | bytes 3076
  0.7 10.5 %copy-start.6 = (s32[8,128]{1,0:T(8,128)S(1)}, s32[8,128]{1,0:T(8,128)}, u32[]{:S(2)}) copy-start(s32[8,128]{1,0:T(8,128)} %param.14) | copy-start | bytes 12292
  0.7 10.5 %copy-start.5 = (f32[2,8,384]{2,1,0:T(8,128)S(1)}, f32[2,8,384]{2,1,0:T(8,128)}, u32[]{:S(2)}) copy-start(f32[2,8,384]{2,1,0:T(8,128)} %param.19) | copy-start | bytes 73732
  0.7 11.1 %copy-start.10 = (f32[256]{0:T(256)S(1)}, f32[256]{0:T(256)}, u32[]{:S(2)}) copy-start(f32[256]{0:T(256)} %param.18) | copy-start | bytes 3076
  5.5 19.2 %collective-permute-start = (bf16[2,384,256]{2,1,0:T(8,128)(2,1)}, bf16[2,384,256]{2,1,0:T(8,128)(2,1)S(1)}, u32[]{:S(2)}, u32[]{:S(2)}) collective-permute-start(bf16[2,384,256]{2,1,0:T(8,128)(2,1)} %get-tuple-element.17), channel_id=1, source_target_pairs={{0,1},{1,0},{2,3},{3,2},{4,5},{5,4},{6,7},{7,6},{8,9},{9,8},{10,11... | collective-permute-start | bytes 1179656 | tf_op jit(solution)/shard_map/ppermute | solution.py:34
  5.9 18.8 %collective-permute-start.1 = (bf16[2,384,256]{2,1,0:T(8,128)(2,1)}, bf16[2,384,256]{2,1,0:T(8,128)(2,1)S(1)}, u32[]{:S(2)}, u32[]{:S(2)}) collective-permute-start(bf16[2,384,256]{2,1,0:T(8,128)(2,1)} %get-tuple-element.18), channel_id=1, source_target_pairs={{1,2},{3,4},{5,6},{7,8},{9,10},{11,12},{13,14},{15,16},{17,18},{19... | collective-permute-start | bytes 1179656 | tf_op jit(solution)/shard_map/ppermute | solution.py:34
  6.6 26.2 %collective-permute-start.2 = (bf16[2,384,256]{2,1,0:T(8,128)(2,1)}, bf16[2,384,256]{2,1,0:T(8,128)(2,1)S(1)}, u32[]{:S(2)}, u32[]{:S(2)}) collective-permute-start(bf16[2,384,256]{2,1,0:T(8,128)(2,1)} %get-tuple-element.19), channel_id=1, source_target_pairs={{0,2},{1,3},{2,0},{3,1},{4,6},{5,7},{6,4},{7,5},{8,10},{9,11},{10,... | collective-permute-start | bytes 1179656 | tf_op jit(solution)/shard_map/ppermute | solution.py:34
  10.4 22.4 %collective-permute-start.3 = (bf16[2,384,256]{2,1,0:T(8,128)(2,1)S(1)}, bf16[2,384,256]{2,1,0:T(8,128)(2,1)S(1)}, u32[]{:S(2)}, u32[]{:S(2)}) collective-permute-start(bf16[2,384,256]{2,1,0:T(8,128)(2,1)S(1)} %get-tuple-element.20), channel_id=1, source_target_pairs={{2,4},{3,5},{6,8},{7,9},{10,12},{11,13},{14,16},{15,17},{18,20},{1... | collective-permute-start | bytes 1179656 | tf_op jit(solution)/shard_map/ppermute | solution.py:34
  12.8 4.5 %copy-start.1 = (bf16[8,384,256]{2,1,0:T(8,128)(2,1)S(1)}, bf16[8,384,256]{2,1,0:T(8,128)(2,1)}, u32[]{:S(2)}) copy-start(bf16[8,384,256]{2,1,0:T(8,128)(2,1)} %refs_2_.3) | copy-start | bytes 4718596
  12.8 4.5 %copy-start.2 = (s32[1,4,2]{2,1,0:T(4,128)S(1)}, s32[1,4,2]{2,1,0:T(4,128)}, u32[]{:S(2)}) copy-start(s32[1,4,2]{2,1,0:T(4,128)} %copy.44.halo.refs_1_) | copy-start | bytes 100
  12.8 4.5 %copy-start.3 = (s32[8,6]{1,0:T(8,128)S(1)}, s32[8,6]{1,0:T(8,128)}, u32[]{:S(2)}) copy-start(s32[8,6]{1,0:T(8,128)} %refs_0_.7) | copy-start | bytes 580
  17.4 5.0 %copy-start = (bf16[8,6,384,384]{3,2,1,0:T(8,128)(2,1)S(1)}, bf16[8,6,384,384]{3,2,1,0:T(8,128)(2,1)}, u32[]{:S(2)}) copy-start(bf16[8,6,384,384]{3,2,1,0:T(8,128)(2,1)} %refs_3_.7) | copy-start | bytes 42467332
  22.4 22.6 %slice-start = ((s8[14155776]{0:T(1024)(128)(4,1)}), s8[4194304]{0:T(1024)(128)(4,1)S(1)}, s32[]{:S(2)}) async-start(s8[14155776]{0:T(1024)(128)(4,1)} %bitcast.13), calls=%async_computation.1 | async-start | bytes 8388608
  22.4 22.6 %slice-start.1 = ((s8[14155776]{0:T(1024)(128)(4,1)}), s8[4194304]{0:T(1024)(128)(4,1)S(1)}, s32[]{:S(2)}) async-start(s8[14155776]{0:T(1024)(128)(4,1)} %bitcast.13), calls=%async_computation.2 | async-start | bytes 8388608
  24.7 20.4 %slice-start.2 = ((s8[14155776]{0:T(1024)(128)(4,1)}), s8[4194304]{0:T(1024)(128)(4,1)S(1)}, s32[]{:S(2)}) async-start(s8[14155776]{0:T(1024)(128)(4,1)} %bitcast.13), calls=%async_computation.3 | async-start | bytes 8388608
  24.7 20.3 %slice-start.3 = ((s8[14155776]{0:T(1024)(128)(4,1)}), s8[1572864]{0:T(1024)(128)(4,1)S(1)}, s32[]{:S(2)}) async-start(s8[14155776]{0:T(1024)(128)(4,1)} %bitcast.13), calls=%async_computation.4 | async-start | bytes 3145728
  35.3 12.2 %collective-permute-start.4 = (bf16[2,384,256]{2,1,0:T(8,128)(2,1)S(1)}, bf16[2,384,256]{2,1,0:T(8,128)(2,1)S(1)}, u32[]{:S(2)}, u32[]{:S(2)}) collective-permute-start(bf16[2,384,256]{2,1,0:T(8,128)(2,1)S(1)} %get-tuple-element.22), channel_id=1, source_target_pairs={{0,1},{1,0},{2,3},{3,2},{4,5},{5,4},{6,7},{7,6},{8,9},{9,8},{10,11... | collective-permute-start | bytes 1179656 | tf_op jit(solution)/shard_map/ppermute | solution.py:34
  39.1 8.5 %collective-permute-start.5 = (bf16[2,384,256]{2,1,0:T(8,128)(2,1)S(1)}, bf16[2,384,256]{2,1,0:T(8,128)(2,1)S(1)}, u32[]{:S(2)}, u32[]{:S(2)}) collective-permute-start(bf16[2,384,256]{2,1,0:T(8,128)(2,1)S(1)} %get-tuple-element.23), channel_id=1, source_target_pairs={{1,2},{3,4},{5,6},{7,8},{9,10},{11,12},{13,14},{15,16},{17,18},{19... | collective-permute-start | bytes 1179656 | tf_op jit(solution)/shard_map/ppermute | solution.py:34
  39.8 24.4 %collective-permute-start.6 = (bf16[2,384,256]{2,1,0:T(8,128)(2,1)S(1)}, bf16[2,384,256]{2,1,0:T(8,128)(2,1)S(1)}, u32[]{:S(2)}, u32[]{:S(2)}) collective-permute-start(bf16[2,384,256]{2,1,0:T(8,128)(2,1)S(1)} %get-tuple-element.24), channel_id=1, source_target_pairs={{0,2},{1,3},{2,0},{3,1},{4,6},{5,7},{6,4},{7,5},{8,10},{9,11},{10,... | collective-permute-start | bytes 1179656 | tf_op jit(solution)/shard_map/ppermute | solution.py:34
  44.3 19.9 %collective-permute-start.7 = (bf16[2,384,256]{2,1,0:T(8,128)(2,1)S(1)}, bf16[2,384,256]{2,1,0:T(8,128)(2,1)S(1)}, u32[]{:S(2)}, u32[]{:S(2)}) collective-permute-start(bf16[2,384,256]{2,1,0:T(8,128)(2,1)S(1)} %get-tuple-element.25), channel_id=1, source_target_pairs={{2,4},{3,5},{6,8},{7,9},{10,12},{11,13},{14,16},{15,17},{18,20},{1... | collective-permute-start | bytes 1179656 | tf_op jit(solution)/shard_map/ppermute | solution.py:34
  67.6 19.1 %all-to-all-start = ((f32[32,1,256]{2,1,0:T(1,128)}), f32[32,1,256]{2,1,0:T(1,128)S(1)}, u32[]{:S(2)}, u32[]{:S(2)}) async-start(f32[32,1,256]{2,1,0:T(1,128)} %get-tuple-element.30), calls=%async_computation | async-start | bytes 65536 | tf_op jit(solution)/shard_map/all_to_all | solution.py:280
  86.6 0.6 copy-start.4

commit v3 on v2

v3 whole, which is shorter than its diff:
```python
import functools

import jax
import jax.numpy as jnp
from jax import lax
from jax.experimental import pallas as pl
from jax.experimental.pallas import tpu as pltpu
from jax.sharding import PartitionSpec as P

PARTS = 2
PICK_COST = (4 << 20, 96 << 20)
EARLY_COST = 4 << 20
LATE_COST = ((4 << 20, 4 << 20), (4 << 20, 4 << 20))
ROUTES = ("swap", "cross", "inner", "outer")


def route_pairs(devices):
    swap = [(i, i ^ 1) for i in range(devices)]
    cross = [(i, i + 1) for i in range(1, devices - 1, 2)]
    inner = [(i, i ^ 2) for i in range(devices)]
    outer = [(i, i + 2) for i in range(devices - 2) if i & 2]
    both = lambda pairs: pairs + [(j, i) for i, j in pairs]
    return dict(swap=swap, cross=both(cross), inner=inner, outer=both(outer))


def send_groups(device):
    core, chip = device % 2, (device // 2) % 2
    return dict(swap=2 - core, cross=1 + core, inner=3 - 3 * chip, outer=3 * chip)


def receive_groups(device):
    core, chip = device % 2, (device // 2) % 2
    return dict(swap=1 + core, cross=2 - core, inner=3 * chip, outer=3 - 3 * chip)


def exchange(sends):
    pairs = route_pairs(lax.axis_size("dom"))
    return {r: lax.ppermute(sends[r], "dom", pairs[r]) for r in ("inner", "cross", "outer", "swap")}


def pinned(value):
    return pltpu.with_memory_space_constraint(value, pltpu.VMEM)


def in_hbm(value):
    return pltpu.with_memory_space_constraint(value, pltpu.HBM)


def pick_kernel(part, halo, lam, *rest):
    outs, sems = dict(zip(ROUTES, rest[:4])), rest[4]
    groups = send_groups(lax.axis_index("dom"))
    copies = []
    for i, r in enumerate(ROUTES):
        for c in range(2):
            row = jnp.maximum(halo[0, c, groups[r]], 0)
            copies.append(
                pltpu.make_async_copy(lam.at[row, :, pl.ds(*part)], outs[r].at[c], sems.at[i, c])
            )
    for copy in copies:
        copy.start()
    for copy in copies:
        copy.wait()


def pick_sends(part, cost, halo, lam):
    sent = pltpu.VMEM((2, lam.shape[1], part[1]), lam.dtype)
    outs = pl.pallas_call(
        functools.partial(pick_kernel, part),
        name="pick_sends",
        out_shape=[sent] * 4,
        in_specs=[pl.BlockSpec(memory_space=pltpu.SMEM), pl.BlockSpec(memory_space=pltpu.HBM)],
        out_specs=[pl.BlockSpec(memory_space=pltpu.VMEM)] * 4,
        scratch_shapes=[pltpu.SemaphoreType.DMA((4, 2))],
        compiler_params=pltpu.CompilerParams(vmem_limit_bytes=4 * 1024 * 1024),
        cost_estimate=pl.CostEstimate(flops=0, bytes_accessed=cost, transcendentals=0),
    )(halo, lam)
    return dict(zip(ROUTES, outs))


def lay_out_facts(facts, aux, gauges):
    wet, snapshots = facts[:2]
    owned, cells = wet.shape
    for i, fact in enumerate(facts[2:]):
        gauges[i : i + 1, :] = fact[...].astype(jnp.float32)
    for b in range(owned):
        rows = [wet[b : b + 1, :].astype(jnp.float32)]
        for t in range(snapshots.shape[0]):
            for c in range(3):
                rows.append(snapshots[t, b : b + 1, c * cells : (c + 1) * cells])
        rows.append(jnp.zeros((1, cells), jnp.float32))
        aux[b] = jnp.concatenate(rows, axis=0).T


def step_kernel(late, last, step, part, final, *refs):
    refs = list(refs)
    take = lambda n: [refs.pop(0) for _ in range(n)]
    cols, halo, lam, ops = take(4)
    begin = not late and step == 0
    facts = take(6) if begin else None
    aux, gauges = (None, None) if begin else take(2)
    received = take(4) if late else []
    take(1 + last if late else 0)
    done_squares = take(1)[0] if late and last else None
    (new,) = take(1)
    raw, squares = take(2) if last else (None, None)
    sends = dict(zip(ROUTES, take(4))) if late and not last else {}
    if begin:
        aux, gauges, kept, op_sem = take(4)
        far, ops = ops, kept
    (slots,) = refs if late else (None,)

    owned, entries = ops.shape[0], ops.shape[1]
    rows, width = lam.shape[1], part[1]
    cells = rows // 3
    here = pl.ds(*part)
    position = lax.axis_index("dom")

    if late:
        groups = receive_groups(position)
        for i, r in enumerate(ROUTES):
            slots[pl.ds(2 * groups[r], 2)] = received[i][...]
    if last:
        if late:
            squares[...] = jnp.broadcast_to(done_squares[...], squares.shape)
        else:
            squares[...] = jnp.zeros(squares.shape, jnp.float32)

    def fetch(b, p):
        pair = pl.ds(2 * p, 2)
        return pltpu.make_async_copy(far.at[b, pair], ops.at[b, pair], op_sem.at[b, p])

    def for_pairs(b, act):
        number = shape_of(b)[0]
        for p in range(entries // 2):

            @pl.when(number > p)
            def _(p=p):
                act(fetch(b, p))

    def shape_of(b):
        live, top = 0, -1
        for k in range(entries):
            live = live + (cols[b, k] >= 0).astype(jnp.int32)
            top = jnp.maximum(top, cols[b, k])
        return (live + 1) // 2, (top >= owned) if late else (top < owned)

    if begin:

        @pl.loop(0, owned)
        def _(b):
            for_pairs(b, lambda copy: copy.start())

        lay_out_facts(facts, aux, gauges)

    first = gauges[1:2, here]
    active = jnp.where(
        jnp.logical_and(first <= step, step < first + gauges[2:3, here]), gauges[3:4, here], 0.0
    )
    own_cells = lax.broadcasted_iota(jnp.int32, (cells, width), 0)

    def finish(b, total):
        wet = aux[b, :, 0:1]
        where = gauges[0:1, here].astype(jnp.int32) - (position * owned + b) * cells
        source = jnp.where(own_cells == where, active, 0.0)
        gathered = None
        for c in range(3):
            band = pl.ds(c * cells, cells)
            before = lam[b, band, here].astype(jnp.float32)
            updated = wet * (before + total[c * cells : (c + 1) * cells])
            if c == 0:
                updated = updated + source
            updated = updated.astype(jnp.bfloat16)
            new[b, band, here] = updated
            if last:
                term = aux[b, :, 1 + c : 2 + c] * before
                gathered = term if gathered is None else gathered + term
                gathered = gathered + aux[b, :, 4 + c : 5 + c] * updated.astype(jnp.float32)
        if last:
            raw[b, :, here] = gathered
            more = jnp.sum(gathered * gathered, axis=0, keepdims=True)[None]
            squares[:, :, here] += jnp.broadcast_to(more, (squares.shape[0], 1, width))

    def picked(b, k):
        col = cols[b, k]
        block = lam[jnp.clip(col, 0, owned - 1), :, here]
        if late:
            block = jnp.where(col < owned, block, slots[jnp.maximum(col - owned, 0)])
        return jnp.where(col >= 0, block, jnp.zeros_like(block))

    def make_row(b, n):
        state = [lam[b, :, here]] + [picked(b, k) for k in range(1, 2 * n)]
        weights = jnp.concatenate([ops[b, k] for k in range(2 * n)], axis=1)
        total = jnp.dot(
            weights, jnp.concatenate(state, axis=0), preferred_element_type=jnp.float32
        )
        finish(b, total)

    def each_row():
        @pl.loop(0, owned)
        def _(b):
            pairs, mine = shape_of(b)
            if begin:
                for_pairs(b, lambda copy: copy.wait())
            for n in range(1, entries // 2 + 1):

                @pl.when(jnp.logical_and(mine, pairs == n))
                def _(n=n):
                    make_row(b, n)

    if late:
        plain = True
        for b in range(owned):
            pairs, mine = shape_of(b)
            plain = jnp.logical_and(plain, jnp.logical_and(mine, pairs == 1))

        @pl.when(plain)
        def _():
            for b in range(owned):
                make_row(b, 1)

        @pl.when(jnp.logical_not(plain))
        def _():
            each_row()
    else:
        each_row()

    if sends:
        groups = send_groups(position)
        for r in ROUTES:
            for c in range(2):
                sends[r][c] = new[jnp.maximum(halo[0, c, groups[r]], 0), :, here]


def step_rows(late, last, step, part, final, cost, inputs, lam, received=None, before=None):
    cols, halo, ops, facts = inputs
    owned, rows, width = lam.shape
    cells = rows // 3
    devices = lax.axis_size("dom")
    smem, vmem = (pl.BlockSpec(memory_space=m) for m in (pltpu.SMEM, pltpu.VMEM))
    begin = not late and step == 0
    args = [cols, halo, pinned(lam), in_hbm(ops) if begin else pinned(ops), *facts]
    aliases = {}
    if late:
        args += [pinned(received[r]) for r in ROUTES]
        for i in range(1 + last):
            aliases[len(args)] = i
            args.append(pinned(before[i]))
        if last:
            args.append(before[2])
    out_shape = [pltpu.VMEM(lam.shape, lam.dtype)]
    if last:
        out_shape += [
            pltpu.VMEM((owned, cells, width), jnp.float32),
            pltpu.VMEM((devices if final else 1, 1, width), jnp.float32),
        ]
    elif late:
        out_shape += [pltpu.VMEM((2, rows, part[1]), lam.dtype)] * 4
    scratch = [pltpu.VMEM((owned, rows, part[1]), lam.dtype)] if late else []
    if begin:
        scratch = [pltpu.SemaphoreType.DMA((owned, ops.shape[1] // 2))]
        out_shape += [
            pltpu.VMEM((owned, cells, 2 + 3 * 2), jnp.float32),
            pltpu.VMEM((4, width), jnp.float32),
            pltpu.VMEM(ops.shape, ops.dtype),
        ]
    return pl.pallas_call(
        functools.partial(step_kernel, late, last, step, part, final),
        name=("late" if late else "early") + "_rows",
        out_shape=out_shape,
        in_specs=[smem, smem, vmem, pl.BlockSpec(memory_space=pltpu.HBM) if begin else vmem]
        + [vmem] * (len(args) - 4),
        out_specs=[vmem] * len(out_shape),
        input_output_aliases=aliases,
        scratch_shapes=scratch,
        compiler_params=pltpu.CompilerParams(vmem_limit_bytes=16 * 1024 * 1024),
        cost_estimate=pl.CostEstimate(flops=0, bytes_accessed=cost, transcendentals=0),
    )(*args)


def scale_kernel(cells_total, sums, raw, out, scaled_rows, sems):
    factor = lax.rsqrt(jnp.sum(sums[...], axis=0) / cells_total + 1e-06)
    copies = []
    for b in range(raw.shape[0]):
        scaled_rows[b] = raw[b] * factor
        copies.append(pltpu.make_async_copy(scaled_rows.at[b], out.at[b], sems.at[b]))
        copies[b].start()
    for copy in copies:
        copy.wait()


def scaled(sums, raw, cells_total):
    vmem = pl.BlockSpec(memory_space=pltpu.VMEM)
    return pl.pallas_call(
        functools.partial(scale_kernel, cells_total),
        name="scale",
        out_shape=jax.ShapeDtypeStruct(raw.shape, raw.dtype),
        in_specs=[vmem, vmem],
        out_specs=pl.BlockSpec(memory_space=pltpu.HBM),
        scratch_shapes=[
            pltpu.VMEM(raw.shape, raw.dtype),
            pltpu.SemaphoreType.DMA((raw.shape[0],)),
        ],
        compiler_params=pltpu.CompilerParams(vmem_limit_bytes=8 * 1024 * 1024),
    )(sums, pinned(raw))


def per_device(
    adjoint_end,
    operator_blocks,
    block_cols,
    halo_send,
    wet_cells,
    gauge_cells,
    window_first,
    window_len,
    gauge_gain,
    snapshots,
):
    owned, cells = wet_cells.shape
    steps = snapshots.shape[0]
    devices = lax.axis_size("dom")
    halo = jnp.swapaxes(halo_send, 1, 2)
    facts = [wet_cells, snapshots] + [
        v[None] for v in (gauge_cells, window_first, window_len, gauge_gain)
    ]
    width = adjoint_end.shape[2]
    parts = [(at, width // PARTS) for at in range(0, width, width // PARTS)]
    lam = adjoint_end
    received = [
        exchange(pick_sends(part, cost, halo, lam)) for part, cost in zip(parts, PICK_COST)
    ]
    for step in range(steps):
        last = step == steps - 1
        inputs = (block_cols, halo, operator_blocks, facts)
        state = step_rows(False, last, step, (0, width), False, EARLY_COST, inputs, lam)
        if step == 0:
            *state, aux, gauges, operator_blocks = state
            facts = [aux, gauges]
            inputs = (block_cols, halo, operator_blocks, facts)
        arriving, received = received, []
        for i, part in enumerate(parts):
            final = last and i == len(parts) - 1
            state = step_rows(
                True, last, step, part, final, LATE_COST[step][i], inputs, lam, arriving[i], state
            )
            if not last:
                received.append(exchange(dict(zip(ROUTES, state[1:]))))
        lam = state[0]
    raw, squares = state[1:]
    sums = lax.all_to_all(squares, "dom", 0, 0, tiled=True)
    return (lam, scaled(sums, raw, devices * owned * cells))


def solution(mesh):
    return jax.shard_map(
        per_device,
        mesh=mesh,
        in_specs=(
            P("dom", None, None),
            P("dom", None, None, None),
            P("dom", None),
            P("dom", None, None),
            P("dom", None),
            P(),
            P(),
            P(),
            P(),
            P(None, "dom", None),
        ),
        out_specs=(P("dom", None, None), P("dom", None, None)),
        check_vma=False,
    )
```

time: 89.6 us -> 79.2 us (0.88)
  waiting for transfers between devices: 30.8 us -> 13.5 us
  starting transfers between devices: 27 us -> 40.9 us
  local copies, waits for them, and re-layouts: 12.7 us -> 3.26 us
  Pallas kernels: 15.9 us -> 19.9 us
  other arithmetic: 1.72 us -> 0 us
    ppermute x8 -> x16, starting transfers between devices: 15.2 us -> 33.1 us  [exchange(): lax.ppermute(sends[r], 'dom', pairs[r])]
    ppermute x8 -> x16, waiting for transfers between devices: 24.7 us -> 7.36 us  [exchange(): lax.ppermute(sends[r], 'dom', pairs[r])]
    unnamed x32 -> x23, local copies, waits for them, and re-layouts: 8.21 us -> 3.26 us
    pallas_call x5 -> x8, Pallas kernels: 14.1 us -> 18.9 us  [the longest x6 17.2 us: step_rows(): pl.pallas_call(functools.partial(step_kernel, late, last, step, part, fin...]
    all_to_all x1, starting transfers between devices: 11.8 us -> 7.8 us  [per_device(): sums = lax.all_to_all(squares, 'dom', 0, 0, tiled=True)]
    another operation x3 -> x0, local copies, waits for them, and re-layouts: 3.35 us -> none  [per_device(): snapshots[t].reshape(owned, 3, cells)]
    transpose x1 -> x0, other arithmetic: 1.69 us -> none  [per_device(): aux = jnp.swapaxes(factors, 1, 2)]
    broadcast_in_dim x1 -> x0, local copies, waits for them, and re-layouts: 1.02 us -> none  [per_device(): wet_cells.astype(jnp.float32)[:, None]]
  transfers between devices with their start and end apart: 9 -> 17, of which waited for: 3 -> 2; matrix products, arithmetic and copies ran while one was open for 8% -> 1% of each run, Pallas kernels for 5% -> 19%
where the time goes in v3:
time: 79.2 us; the launch traced here: 78.7 us
  starting transfers between devices  40.9 us (52%)
  Pallas kernels  19.9 us (25%)
  waiting for transfers between devices  13.5 us (17%)
  local copies, waits for them, and re-layouts  3.26 us (4%)
  between operations  1.12 us (1%)
    ppermute x16, starting transfers between devices, exchange(): lax.ppermute(sends[r], 'dom', pairs[r])  33.1 us
    pallas_call x6, Pallas kernels, step_rows(): pl.pallas_call(functools.partial(step_kernel, late, last, step, part, fin...  17.2 us
    all_to_all x1, starting transfers between devices, per_device(): sums = lax.all_to_all(squares, 'dom', 0, 0, tiled=True)  7.8 us
    ppermute x16, waiting for transfers between devices, exchange(): lax.ppermute(sends[r], 'dom', pairs[r])  7.36 us
    all_to_all x1, waiting for transfers between devices, per_device(): sums = lax.all_to_all(squares, 'dom', 0, 0, tiled=True)  6.1 us
    unnamed x23, local copies, waits for them, and re-layouts  3.26 us
    pallas_call x2, Pallas kernels, pick_sends(): pl.pallas_call(functools.partial(pick_kernel, part), name='pick_sends', o...  1.62 us
  transfers between devices with their start and end apart: 17, of which 2 were waited for; matrix products, arithmetic and copies ran while one was open for 1% of the time, Pallas kernels for 19%

profile of v3, /device:TPU:0, one launch (start us, length us, event | category | flops | bytes accessed | tf_op | source)
XLA Modules:
  0.0 78.7 jit_solution(6907468387874286466)
XLA Ops:
  0.6 1.4 %copy-done = bf16[8,384,256]{2,1,0:T(8,128)(2,1)S(1)} copy-done((bf16[8,384,256]{2,1,0:T(8,128)(2,1)S(1)}, bf16[8,384,256]{2,1,0:T(8,128)(2,1)}, u32[]{:S(2)}) %copy-start) | copy-done | bytes 1572888
  2.0 0.7 copy-done.3
  2.8 0.8 %pick_sends.3 = (bf16[2,384,128]{2,1,0:T(8,128)(2,1)S(1)}, bf16[2,384,128]{2,1,0:T(8,128)(2,1)S(1)}, bf16[2,384,128]{2,1,0:T(8,128)(2,1)S(1)}, bf16[2,384,128]{2,1,0:T(8,128)(2,1)S(1)}) custom-call(s32[1,2,4]{2,1,0:T(2,128)S(1)} %bitcast.5, bf16[8,384,256]{2,1,0:T(8,128)(2,1)S(1)} %copy-done), custom_call_target="tpu_custom_call" | custom-call | bytes 4194304 | tf_op jit(solution)/shard_map/pick_sends/pallas_call | solution.py:67
  3.6 0.5 collective-permute-start.4
  4.1 0.7 collective-permute-start.5
  4.8 3.8 %collective-permute-start.6 = (bf16[2,384,128]{2,1,0:T(8,128)(2,1)S(1)}, bf16[2,384,128]{2,1,0:T(8,128)(2,1)S(1)}, u32[]{:S(2)}, u32[]{:S(2)}) collective-permute-start(bf16[2,384,128]{2,1,0:T(8,128)(2,1)S(1)} %get-tuple-element.42), channel_id=1, source_target_pairs={{0,2},{1,3},{2,0},{3,1},{4,6},{5,7},{6,4},{7,5},{8,10},{9,11},{10,... | collective-permute-start | bytes 589832 | tf_op jit(solution)/shard_map/ppermute | solution.py:38
  8.6 0.7 collective-permute-start.7
  9.3 0.8 %pick_sends.2 = (bf16[2,384,128]{2,1,0:T(8,128)(2,1)S(1)}, bf16[2,384,128]{2,1,0:T(8,128)(2,1)S(1)}, bf16[2,384,128]{2,1,0:T(8,128)(2,1)S(1)}, bf16[2,384,128]{2,1,0:T(8,128)(2,1)S(1)}) custom-call(s32[1,2,4]{2,1,0:T(2,128)S(1)} %bitcast.6, bf16[8,384,256]{2,1,0:T(8,128)(2,1)S(1)} %copy-done), custom_call_target="tpu_custom_call" | custom-call | bytes 100663296 | tf_op jit(solution)/shard_map/pick_sends/pallas_call | solution.py:67
  10.1 1.4 %collective-permute-start = (bf16[2,384,128]{2,1,0:T(8,128)(2,1)S(1)}, bf16[2,384,128]{2,1,0:T(8,128)(2,1)S(1)}, u32[]{:S(2)}, u32[]{:S(2)}) collective-permute-start(bf16[2,384,128]{2,1,0:T(8,128)(2,1)S(1)} %get-tuple-element.36), channel_id=1, source_target_pairs={{0,1},{1,0},{2,3},{3,2},{4,5},{5,4},{6,7},{7,6},{8,9},{9,8},{10,11... | collective-permute-start | bytes 589832 | tf_op jit(solution)/shard_map/ppermute | solution.py:38
  11.5 0.7 collective-permute-start.1
  12.2 4.1 %early_rows.2 = (bf16[8,384,256]{2,1,0:T(8,128)(2,1)S(1)}, f32[8,128,8]{2,1,0:T(8,128)S(1)}, f32[4,256]{1,0:T(4,128)S(1)}, bf16[8,6,384,384]{3,2,1,0:T(8,128)(2,1)S(1)}) custom-call(s32[8,6]{1,0:T(8,128)S(1)} %copy-done.2, s32[1,2,4]{2,1,0:T(2,128)S(1)} %bitcast.7, bf16[8,384,256]{2,1,0:T(8,128)(2,1)S(1)} %copy-done.1, bf16[8,6,384,384]{3,2,1,0:T(8,128)(2,1)} %refs_3_.1, ...), custom_call_target="tpu_custom_call" | custom-call | bytes 4194304 | tf_op jit(solution)/shard_map/early_rows/pallas_call | solution.py:266
  16.3 5.1 %collective-permute-start.2 = (bf16[2,384,128]{2,1,0:T(8,128)(2,1)S(1)}, bf16[2,384,128]{2,1,0:T(8,128)(2,1)S(1)}, u32[]{:S(2)}, u32[]{:S(2)}) collective-permute-start(bf16[2,384,128]{2,1,0:T(8,128)(2,1)S(1)} %get-tuple-element.38), channel_id=1, source_target_pairs={{0,2},{1,3},{2,0},{3,1},{4,6},{5,7},{6,4},{7,5},{8,10},{9,11},{10,... | collective-permute-start | bytes 589832 | tf_op jit(solution)/shard_map/ppermute | solution.py:38
  21.4 0.0 collective-permute-done.6.refs_8_
  21.4 0.7 collective-permute-start.3
  22.1 2.5 %late_rows.4 = (bf16[8,384,256]{2,1,0:T(8,128)(2,1)S(1)}, bf16[2,384,128]{2,1,0:T(8,128)(2,1)S(1)}, bf16[2,384,128]{2,1,0:T(8,128)(2,1)S(1)}, bf16[2,384,128]{2,1,0:T(8,128)(2,1)S(1)}, bf16[2,384,128]{2,1,0:T(8,128)(2,1)S(1)}) custom-call(s32[8,6]{1,0:T(8,128)S(1)} %copy-done.2, s32[1,2,4]{2,1,0:T(2,128)S(1)} %bitcast.8, ...), custom_call_target="tpu_custom_call", output_to_operand_aliasing={{0}: (10, {})} | custom-call | bytes 4194304 | tf_op jit(solution)/shard_map/late_rows/pallas_call | solution.py:266
  24.6 3.9 %collective-permute-start.12 = (bf16[2,384,128]{2,1,0:T(8,128)(2,1)S(1)}, bf16[2,384,128]{2,1,0:T(8,128)(2,1)S(1)}, u32[]{:S(2)}, u32[]{:S(2)}) collective-permute-start(bf16[2,384,128]{2,1,0:T(8,128)(2,1)S(1)} %get-tuple-element.51), channel_id=1, source_target_pairs={{0,1},{1,0},{2,3},{3,2},{4,5},{5,4},{6,7},{7,6},{8,9},{9,8},{10,11... | collective-permute-start | bytes 589832 | tf_op jit(solution)/shard_map/ppermute | solution.py:38
  28.5 0.7 collective-permute-start.13
  29.2 6.7 %collective-permute-start.14 = (bf16[2,384,128]{2,1,0:T(8,128)(2,1)S(1)}, bf16[2,384,128]{2,1,0:T(8,128)(2,1)S(1)}, u32[]{:S(2)}, u32[]{:S(2)}) collective-permute-start(bf16[2,384,128]{2,1,0:T(8,128)(2,1)S(1)} %get-tuple-element.53), channel_id=1, source_target_pairs={{0,2},{1,3},{2,0},{3,1},{4,6},{5,7},{6,4},{7,5},{8,10},{9,11},{10,... | collective-permute-start | bytes 589832 | tf_op jit(solution)/shard_map/ppermute | solution.py:38
  35.9 2.5 %late_rows.5 = (bf16[8,384,256]{2,1,0:T(8,128)(2,1)S(1)}, bf16[2,384,128]{2,1,0:T(8,128)(2,1)S(1)}, bf16[2,384,128]{2,1,0:T(8,128)(2,1)S(1)}, bf16[2,384,128]{2,1,0:T(8,128)(2,1)S(1)}, bf16[2,384,128]{2,1,0:T(8,128)(2,1)S(1)}) custom-call(s32[8,6]{1,0:T(8,128)S(1)} %copy-done.2, s32[1,2,4]{2,1,0:T(2,128)S(1)} %bitcast.9, ...), custom_call_target="tpu_custom_call", output_to_operand_aliasing={{0}: (10, {})} | custom-call | bytes 4194304 | tf_op jit(solution)/shard_map/late_rows/pallas_call | solution.py:266
  38.3 0.7 collective-permute-start.8
  39.1 0.7 collective-permute-start.15
  39.7 0.7 collective-permute-start.9
  40.4 5.7 %collective-permute-start.10 = (bf16[2,384,128]{2,1,0:T(8,128)(2,1)S(1)}, bf16[2,384,128]{2,1,0:T(8,128)(2,1)S(1)}, u32[]{:S(2)}, u32[]{:S(2)}) collective-permute-start(bf16[2,384,128]{2,1,0:T(8,128)(2,1)S(1)} %get-tuple-element.49), channel_id=1, source_target_pairs={{0,2},{1,3},{2,0},{3,1},{4,6},{5,7},{6,4},{7,5},{8,10},{9,11},{10,... | collective-permute-start | bytes 589832 | tf_op jit(solution)/shard_map/ppermute | solution.py:38
  46.1 0.7 collective-permute-start.11
  46.8 2.5 %early_rows.3 = (bf16[8,384,256]{2,1,0:T(8,128)(2,1)S(1)}, f32[8,128,256]{2,1,0:T(8,128)S(1)}, f32[1,1,256]{2,1,0:T(1,128)S(1)}) custom-call(s32[8,6]{1,0:T(8,128)S(1)} %copy-done.2, s32[1,2,4]{2,1,0:T(2,128)S(1)} %bitcast.10, bf16[8,384,256]{2,1,0:T(8,128)(2,1)S(1)} %get-tuple-element.46.refs_2_, bf16[8,6,384,384]{3,2,1,0:T(8,128)(2,1)S(1)} %get-tuple-element.33.refs_3_, ...), custom_call_target="tpu_custom_call" | custom-call | bytes 4194304 | tf_op jit(solution)/shard_map/early_rows/pallas_call | solution.py:266
  49.3 2.6 %late_rows.6 = (bf16[8,384,256]{2,1,0:T(8,128)(2,1)S(1)}, f32[8,128,256]{2,1,0:T(8,128)S(1)}, f32[1,1,256]{2,1,0:T(1,128)S(1)}) custom-call(s32[8,6]{1,0:T(8,128)S(1)} %copy-done.2, s32[1,2,4]{2,1,0:T(2,128)S(1)} %bitcast.11, bf16[8,384,256]{2,1,0:T(8,128)(2,1)S(1)} %get-tuple-element.46.refs_2_, ...), custom_call_target="tpu_custom_call", output_to_operand_aliasing={{0}: (10, {}), {1}: (11, {})} | custom-call | bytes 4194304 | tf_op jit(solution)/shard_map/late_rows/pallas_call | solution.py:266
  51.9 7.3 %collective-permute-done.10.refs_8_ = bf16[2,384,128]{2,1,0:T(8,128)(2,1)S(1)} collective-permute-done((bf16[2,384,128]{2,1,0:T(8,128)(2,1)S(1)}, bf16[2,384,128]{2,1,0:T(8,128)(2,1)S(1)}, u32[]{:S(2)}, u32[]{:S(2)}) %collective-permute-start.10) | collective-permute-done | bytes 196640 | tf_op jit(solution)/shard_map/ppermute | solution.py:38
  59.2 3.1 %late_rows.7 = (bf16[8,384,256]{2,1,0:T(8,128)(2,1)S(1)}, f32[8,128,256]{2,1,0:T(8,128)S(1)}, f32[32,1,256]{2,1,0:T(1,128)}) custom-call(s32[8,6]{1,0:T(8,128)S(1)} %copy-done.2, s32[1,2,4]{2,1,0:T(2,128)S(1)} %bitcast.12, bf16[8,384,256]{2,1,0:T(8,128)(2,1)S(1)} %get-tuple-element.46.refs_2_, ...), custom_call_target="tpu_custom_call", output_to_operand_aliasing={{0}: (10, {}), {1}: (11, {})} | custom-call | bytes 4194304 | tf_op jit(solution)/shard_map/late_rows/pallas_call | solution.py:266
  62.3 7.8 %all-to-all-start = ((f32[32,1,256]{2,1,0:T(1,128)}), f32[32,1,256]{2,1,0:T(1,128)S(1)}, u32[]{:S(2)}, u32[]{:S(2)}) async-start(f32[32,1,256]{2,1,0:T(1,128)} %get-tuple-element.62), calls=%async_computation | async-start | bytes 65536 | tf_op jit(solution)/shard_map/all_to_all | solution.py:350
  70.2 1.1 %copy.24 = bf16[8,384,256]{2,1,0:T(8,128)(2,1)} copy(bf16[8,384,256]{2,1,0:T(8,128)(2,1)S(1)} %get-tuple-element.64) | data formatting | bytes 3145728
  71.3 6.1 %all-to-all-done.sums = f32[32,1,256]{2,1,0:T(1,128)S(1)} async-done(((f32[32,1,256]{2,1,0:T(1,128)}), f32[32,1,256]{2,1,0:T(1,128)S(1)}, u32[]{:S(2)}, u32[]{:S(2)}) %all-to-all-start) | async-done | bytes 32800 | tf_op jit(solution)/shard_map/all_to_all | solution.py:350
  77.4 1.1 %scale.1 = f32[8,128,256]{2,1,0:T(8,128)} custom-call(f32[32,1,256]{2,1,0:T(1,128)S(1)} %all-to-all-done.sums, f32[8,128,256]{2,1,0:T(8,128)S(1)} %get-tuple-element.63.raw), custom_call_target="tpu_custom_call" | custom-call | tf_op jit(solution)/shard_map/scale/pallas_call | solution.py:293
  (34 shorter events, 0.1 us)
Async XLA Ops:
  0.6 1.4 %copy-start = (bf16[8,384,256]{2,1,0:T(8,128)(2,1)S(1)}, bf16[8,384,256]{2,1,0:T(8,128)(2,1)}, u32[]{:S(2)}) copy-start(bf16[8,384,256]{2,1,0:T(8,128)(2,1)} %refs_2_.5) | copy-start | bytes 4718596
  2.0 0.7 copy-start.3
  2.7 9.4 %copy-start.1 = (bf16[8,384,256]{2,1,0:T(8,128)(2,1)S(1)}, bf16[8,384,256]{2,1,0:T(8,128)(2,1)}, u32[]{:S(2)}) copy-start(bf16[8,384,256]{2,1,0:T(8,128)(2,1)} %refs_2_.5) | copy-start | bytes 4718596
  2.7 9.4 %copy-start.2 = (s32[8,6]{1,0:T(8,128)S(1)}, s32[8,6]{1,0:T(8,128)}, u32[]{:S(2)}) copy-start(s32[8,6]{1,0:T(8,128)} %refs_0_.11) | copy-start | bytes 580
  2.7 9.5 %copy-start.4 = (s32[1,4,2]{1,2,0:T(2,128)S(1)}, s32[1,4,2]{1,2,0:T(2,128)}, u32[]{:S(2)}) copy-start(s32[1,4,2]{1,2,0:T(2,128)} %param.13) | copy-start | bytes 100
  2.7 9.5 %copy-start.5 = (f32[2,8,384]{2,1,0:T(8,128)S(1)}, f32[2,8,384]{2,1,0:T(8,128)}, u32[]{:S(2)}) copy-start(f32[2,8,384]{2,1,0:T(8,128)} %refs_5_.1) | copy-start | bytes 73732
  2.7 9.5 %copy-start.6 = (s32[8,128]{1,0:T(8,128)S(1)}, s32[8,128]{1,0:T(8,128)}, u32[]{:S(2)}) copy-start(s32[8,128]{1,0:T(8,128)} %refs_4_.1) | copy-start | bytes 12292
  2.7 9.5 %copy-start.7 = (s32[256]{0:T(256)S(1)}, s32[256]{0:T(256)}, u32[]{:S(2)}) copy-start(s32[256]{0:T(256)} %param.15) | copy-start | bytes 3076
  2.8 9.5 %copy-start.8 = (s32[256]{0:T(256)S(1)}, s32[256]{0:T(256)}, u32[]{:S(2)}) copy-start(s32[256]{0:T(256)} %param.16) | copy-start | bytes 3076
  2.8 9.5 %copy-start.9 = (s32[256]{0:T(256)S(1)}, s32[256]{0:T(256)}, u32[]{:S(2)}) copy-start(s32[256]{0:T(256)} %param.17) | copy-start | bytes 3076
  2.8 9.5 %copy-start.10 = (f32[256]{0:T(256)S(1)}, f32[256]{0:T(256)}, u32[]{:S(2)}) copy-start(f32[256]{0:T(256)} %param.18) | copy-start | bytes 3076
  3.6 7.9 %collective-permute-start.4 = (bf16[2,384,128]{2,1,0:T(8,128)(2,1)S(1)}, bf16[2,384,128]{2,1,0:T(8,128)(2,1)S(1)}, u32[]{:S(2)}, u32[]{:S(2)}) collective-permute-start(bf16[2,384,128]{2,1,0:T(8,128)(2,1)S(1)} %get-tuple-element.40), channel_id=1, source_target_pairs={{0,1},{1,0},{2,3},{3,2},{4,5},{5,4},{6,7},{7,6},{8,9},{9,8},{10,11... | collective-permute-start | bytes 589832 | tf_op jit(solution)/shard_map/ppermute | solution.py:38
  4.1 12.2 %collective-permute-start.5 = (bf16[2,384,128]{2,1,0:T(8,128)(2,1)S(1)}, bf16[2,384,128]{2,1,0:T(8,128)(2,1)S(1)}, u32[]{:S(2)}, u32[]{:S(2)}) collective-permute-start(bf16[2,384,128]{2,1,0:T(8,128)(2,1)S(1)} %get-tuple-element.41), channel_id=1, source_target_pairs={{1,2},{3,4},{5,6},{7,8},{9,10},{11,12},{13,14},{15,16},{17,18},{19... | collective-permute-start | bytes 589832 | tf_op jit(solution)/shard_map/ppermute | solution.py:38
  4.8 16.6 %collective-permute-start.6 = (bf16[2,384,128]{2,1,0:T(8,128)(2,1)S(1)}, bf16[2,384,128]{2,1,0:T(8,128)(2,1)S(1)}, u32[]{:S(2)}, u32[]{:S(2)}) collective-permute-start(bf16[2,384,128]{2,1,0:T(8,128)(2,1)S(1)} %get-tuple-element.42), channel_id=1, source_target_pairs={{0,2},{1,3},{2,0},{3,1},{4,6},{5,7},{6,4},{7,5},{8,10},{9,11},{10,... | collective-permute-start | bytes 589832 | tf_op jit(solution)/shard_map/ppermute | solution.py:38
  8.6 13.5 %collective-permute-start.7 = (bf16[2,384,128]{2,1,0:T(8,128)(2,1)S(1)}, bf16[2,384,128]{2,1,0:T(8,128)(2,1)S(1)}, u32[]{:S(2)}, u32[]{:S(2)}) collective-permute-start(bf16[2,384,128]{2,1,0:T(8,128)(2,1)S(1)} %get-tuple-element.43), channel_id=1, source_target_pairs={{2,4},{3,5},{6,8},{7,9},{10,12},{11,13},{14,16},{15,17},{18,20},{1... | collective-permute-start | bytes 589832 | tf_op jit(solution)/shard_map/ppermute | solution.py:38
  10.1 18.4 %collective-permute-start = (bf16[2,384,128]{2,1,0:T(8,128)(2,1)S(1)}, bf16[2,384,128]{2,1,0:T(8,128)(2,1)S(1)}, u32[]{:S(2)}, u32[]{:S(2)}) collective-permute-start(bf16[2,384,128]{2,1,0:T(8,128)(2,1)S(1)} %get-tuple-element.36), channel_id=1, source_target_pairs={{0,1},{1,0},{2,3},{3,2},{4,5},{5,4},{6,7},{7,6},{8,9},{9,8},{10,11... | collective-permute-start | bytes 589832 | tf_op jit(solution)/shard_map/ppermute | solution.py:38
  11.5 17.7 %collective-permute-start.1 = (bf16[2,384,128]{2,1,0:T(8,128)(2,1)S(1)}, bf16[2,384,128]{2,1,0:T(8,128)(2,1)S(1)}, u32[]{:S(2)}, u32[]{:S(2)}) collective-permute-start(bf16[2,384,128]{2,1,0:T(8,128)(2,1)S(1)} %get-tuple-element.37), channel_id=1, source_target_pairs={{1,2},{3,4},{5,6},{7,8},{9,10},{11,12},{13,14},{15,16},{17,18},{19... | collective-permute-start | bytes 589832 | tf_op jit(solution)/shard_map/ppermute | solution.py:38
  16.3 19.5 %collective-permute-start.2 = (bf16[2,384,128]{2,1,0:T(8,128)(2,1)S(1)}, bf16[2,384,128]{2,1,0:T(8,128)(2,1)S(1)}, u32[]{:S(2)}, u32[]{:S(2)}) collective-permute-start(bf16[2,384,128]{2,1,0:T(8,128)(2,1)S(1)} %get-tuple-element.38), channel_id=1, source_target_pairs={{0,2},{1,3},{2,0},{3,1},{4,6},{5,7},{6,4},{7,5},{8,10},{9,11},{10,... | collective-permute-start | bytes 589832 | tf_op jit(solution)/shard_map/ppermute | solution.py:38
  21.4 14.4 %collective-permute-start.3 = (bf16[2,384,128]{2,1,0:T(8,128)(2,1)S(1)}, bf16[2,384,128]{2,1,0:T(8,128)(2,1)S(1)}, u32[]{:S(2)}, u32[]{:S(2)}) collective-permute-start(bf16[2,384,128]{2,1,0:T(8,128)(2,1)S(1)} %get-tuple-element.39), channel_id=1, source_target_pairs={{2,4},{3,5},{6,8},{7,9},{10,12},{11,13},{14,16},{15,17},{18,20},{1... | collective-permute-start | bytes 589832 | tf_op jit(solution)/shard_map/ppermute | solution.py:38
  24.6 15.2 %collective-permute-start.12 = (bf16[2,384,128]{2,1,0:T(8,128)(2,1)S(1)}, bf16[2,384,128]{2,1,0:T(8,128)(2,1)S(1)}, u32[]{:S(2)}, u32[]{:S(2)}) collective-permute-start(bf16[2,384,128]{2,1,0:T(8,128)(2,1)S(1)} %get-tuple-element.51), channel_id=1, source_target_pairs={{0,1},{1,0},{2,3},{3,2},{4,5},{5,4},{6,7},{7,6},{8,9},{9,8},{10,11... | collective-permute-start | bytes 589832 | tf_op jit(solution)/shard_map/ppermute | solution.py:38
  28.5 11.9 %collective-permute-start.13 = (bf16[2,384,128]{2,1,0:T(8,128)(2,1)S(1)}, bf16[2,384,128]{2,1,0:T(8,128)(2,1)S(1)}, u32[]{:S(2)}, u32[]{:S(2)}) collective-permute-start(bf16[2,384,128]{2,1,0:T(8,128)(2,1)S(1)} %get-tuple-element.52), channel_id=1, source_target_pairs={{1,2},{3,4},{5,6},{7,8},{9,10},{11,12},{13,14},{15,16},{17,18},{19... | collective-permute-start | bytes 589832 | tf_op jit(solution)/shard_map/ppermute | solution.py:38
  29.2 16.9 %collective-permute-start.14 = (bf16[2,384,128]{2,1,0:T(8,128)(2,1)S(1)}, bf16[2,384,128]{2,1,0:T(8,128)(2,1)S(1)}, u32[]{:S(2)}, u32[]{:S(2)}) collective-permute-start(bf16[2,384,128]{2,1,0:T(8,128)(2,1)S(1)} %get-tuple-element.53), channel_id=1, source_target_pairs={{0,2},{1,3},{2,0},{3,1},{4,6},{5,7},{6,4},{7,5},{8,10},{9,11},{10,... | collective-permute-start | bytes 589832 | tf_op jit(solution)/shard_map/ppermute | solution.py:38
  38.3 13.5 %collective-permute-start.8 = (bf16[2,384,128]{2,1,0:T(8,128)(2,1)S(1)}, bf16[2,384,128]{2,1,0:T(8,128)(2,1)S(1)}, u32[]{:S(2)}, u32[]{:S(2)}) collective-permute-start(bf16[2,384,128]{2,1,0:T(8,128)(2,1)S(1)} %get-tuple-element.47), channel_id=1, source_target_pairs={{0,1},{1,0},{2,3},{3,2},{4,5},{5,4},{6,7},{7,6},{8,9},{9,8},{10,11... | collective-permute-start | bytes 589832 | tf_op jit(solution)/shard_map/ppermute | solution.py:38
  39.1 10.2 %collective-permute-start.15 = (bf16[2,384,128]{2,1,0:T(8,128)(2,1)S(1)}, bf16[2,384,128]{2,1,0:T(8,128)(2,1)S(1)}, u32[]{:S(2)}, u32[]{:S(2)}) collective-permute-start(bf16[2,384,128]{2,1,0:T(8,128)(2,1)S(1)} %get-tuple-element.54), channel_id=1, source_target_pairs={{2,4},{3,5},{6,8},{7,9},{10,12},{11,13},{14,16},{15,17},{18,20},{1... | collective-permute-start | bytes 589832 | tf_op jit(solution)/shard_map/ppermute | solution.py:38
  39.7 12.1 %collective-permute-start.9 = (bf16[2,384,128]{2,1,0:T(8,128)(2,1)S(1)}, bf16[2,384,128]{2,1,0:T(8,128)(2,1)S(1)}, u32[]{:S(2)}, u32[]{:S(2)}) collective-permute-start(bf16[2,384,128]{2,1,0:T(8,128)(2,1)S(1)} %get-tuple-element.48), channel_id=1, source_target_pairs={{1,2},{3,4},{5,6},{7,8},{9,10},{11,12},{13,14},{15,16},{17,18},{19... | collective-permute-start | bytes 589832 | tf_op jit(solution)/shard_map/ppermute | solution.py:38
  40.4 18.8 %collective-permute-start.10 = (bf16[2,384,128]{2,1,0:T(8,128)(2,1)S(1)}, bf16[2,384,128]{2,1,0:T(8,128)(2,1)S(1)}, u32[]{:S(2)}, u32[]{:S(2)}) collective-permute-start(bf16[2,384,128]{2,1,0:T(8,128)(2,1)S(1)} %get-tuple-element.49), channel_id=1, source_target_pairs={{0,2},{1,3},{2,0},{3,1},{4,6},{5,7},{6,4},{7,5},{8,10},{9,11},{10,... | collective-permute-start | bytes 589832 | tf_op jit(solution)/shard_map/ppermute | solution.py:38
  46.1 13.1 %collective-permute-start.11 = (bf16[2,384,128]{2,1,0:T(8,128)(2,1)S(1)}, bf16[2,384,128]{2,1,0:T(8,128)(2,1)S(1)}, u32[]{:S(2)}, u32[]{:S(2)}) collective-permute-start(bf16[2,384,128]{2,1,0:T(8,128)(2,1)S(1)} %get-tuple-element.50), channel_id=1, source_target_pairs={{2,4},{3,5},{6,8},{7,9},{10,12},{11,13},{14,16},{15,17},{18,20},{1... | collective-permute-start | bytes 589832 | tf_op jit(solution)/shard_map/ppermute | solution.py:38
  62.3 15.1 %all-to-all-start = ((f32[32,1,256]{2,1,0:T(1,128)}), f32[32,1,256]{2,1,0:T(1,128)S(1)}, u32[]{:S(2)}, u32[]{:S(2)}) async-start(f32[32,1,256]{2,1,0:T(1,128)} %get-tuple-element.62), calls=%async_computation | async-start | bytes 65536 | tf_op jit(solution)/shard_map/all_to_all | solution.py:350
